TPU v7x, 32 devices: a whole 2x2x4 slice. The times are simulated.
32 devices in a mesh: dp: 4 (over y, x), ctx: 8 (over z, core).
Axes of the slice: x: 2, y: 2, z: 4, core: 2. Of those that a mesh axis runs over, the one named last changes fastest.
Arguments:
- tokens: bfloat16 [8, 2048, 2048], P('dp', 'ctx'), may hold values from -6 to 6
- output_grad: bfloat16 [8, 2048, 2048], P('dp', 'ctx'), may hold values from -6 to 6
- segment_ids: int32 [8, 2048], P('dp', 'ctx'), may hold values from 0 to 3, as said below
- positions: int32 [8, 2048], P('dp', 'ctx'), may hold values from 0 to 4095, as said below
- qkv_weight: float32 [2048, 3072], P(('dp', 'ctx')), may hold values from -0.125 to 0.125
- qkv_first: float32 [2048, 3072], P(('dp', 'ctx')), may hold values from -96 to 96
- qkv_second: float32 [2048, 3072], P(('dp', 'ctx')), may hold values from 1185.6842 to 4742.737
- out_weight: float32 [2048, 2048], P(('dp', 'ctx')), may hold values from -1 to 1
- out_first: float32 [2048, 2048], P(('dp', 'ctx')), may hold values from -6 to 6
- out_second: float32 [2048, 2048], P(('dp', 'ctx')), may hold values from 5.4325895 to 21.730358
- gate_up_weight: float32 [2048, 16384], P(('dp', 'ctx')), may hold values from -0.125 to 0.125
- gate_up_first: float32 [2048, 16384], P(('dp', 'ctx')), may hold values from -24 to 24
- gate_up_second: float32 [2048, 16384], P(('dp', 'ctx')), may hold values from 77.60842 to 310.4337
- down_weight: float32 [8192, 2048], P(('dp', 'ctx')), may hold values from -0.0625 to 0.0625
- down_first: float32 [8192, 2048], P(('dp', 'ctx')), may hold values from -48 to 48
- down_second: float32 [8192, 2048], P(('dp', 'ctx')), may hold values from 310.4337 to 1241.7347
- norm_gains: float32 [2, 2048], P(None, ('dp', 'ctx')), may hold values from 0.5 to 1.5
- norm_first: float32 [2, 2048], P(None, ('dp', 'ctx')), may hold values from -96 to 96
- norm_second: float32 [2, 2048], P(None, ('dp', 'ctx')), may hold values from 1185.6842 to 4742.737
- head_gains: float32 [2, 64], replicated, may hold values from 0.5 to 1.5
- head_first: float32 [2, 64], replicated, may hold values from -256 to 256
- head_second: float32 [2, 64], replicated, may hold values from 9485.474 to 37941.895
Outputs:
- outputs: bfloat16 [8, 2048, 2048], P('dp', 'ctx')
- input_grad: bfloat16 [8, 2048, 2048], P('dp', 'ctx')
- new_qkv: float32 [2048, 3072], P(('dp', 'ctx'))
- new_qkv_first: float32 [2048, 3072], P(('dp', 'ctx'))
- new_qkv_second: float32 [2048, 3072], P(('dp', 'ctx'))
- new_out: float32 [2048, 2048], P(('dp', 'ctx'))
- new_out_first: float32 [2048, 2048], P(('dp', 'ctx'))
- new_out_second: float32 [2048, 2048], P(('dp', 'ctx'))
- new_gate_up: float32 [2048, 16384], P(('dp', 'ctx'))
- new_gate_up_first: float32 [2048, 16384], P(('dp', 'ctx'))
- new_gate_up_second: float32 [2048, 16384], P(('dp', 'ctx'))
- new_down: float32 [8192, 2048], P(('dp', 'ctx'))
- new_down_first: float32 [8192, 2048], P(('dp', 'ctx'))
- new_down_second: float32 [8192, 2048], P(('dp', 'ctx'))
- new_norm_gains: float32 [2, 2048], P(None, ('dp', 'ctx'))
- new_norm_first: float32 [2, 2048], P(None, ('dp', 'ctx'))
- new_norm_second: float32 [2, 2048], P(None, ('dp', 'ctx'))
- new_head_gains: float32 [2, 64], replicated
- new_head_first: float32 [2, 64], replicated
- new_head_second: float32 [2, 64], replicated
Inputs may be any that keep to these rules, and one draw needn't show every extreme that they name: `segment_ids`: within each sequence the ids start at 0 and never fall by more than nothing; documents other than a sequence's last hold 204 tokens or more; in each dp index one of its 2 sequences is a single document, and every other sequence holds 4 documents, the first three of 512 tokens at most. `positions`: positions count up by one within a document from 0, except that a sequence's first document may start at a later position.
All inputs are finite; a program needn't handle non-finite values.
Results may differ from a plain program's by a relative error of at most 0.04.
Values may be sent and summed in bfloat16 or wider, within the bound.
A program may use at most 408 MiB of HBM per device.

v0:
```python
import math

import jax
import jax.numpy as jnp
from jax import lax
from jax.sharding import PartitionSpec as P

H = 32
KV = 8
HD = 64
FF = 8192
STEP = 5


EPS = 1e-05
ROPE_BASE = 1000000.0
BETA_ONE = 0.9
BETA_TWO = 0.95
ADAM_EPS = 1e-08
DECAY = 0.1
RATE_QKV = 0.05
RATE_OUT = 0.3
RATE_GATE_UP = 0.05
RATE_DOWN = 0.03
RATE_GAIN = 0.5


def rms_parts(values, gain):
    inv_rms = lax.rsqrt(jnp.mean(values * values, axis=-1, keepdims=True) + EPS)
    return (values * inv_rms * gain, inv_rms)


def norm_back(grad_in, values, inv_rms, gain):
    scaled = grad_in * gain
    inner = jnp.mean(scaled * values, axis=-1, keepdims=True)
    return (inv_rms * (scaled - values * inv_rms * inv_rms * inner), grad_in * values * inv_rms)


def rotary(values, cosine, sine_table):
    half_width = values.shape[-1] // 2
    first_half = values[..., :half_width]
    second_half = values[..., half_width:]
    return jnp.concatenate(
        [
            first_half * cosine - second_half * sine_table,
            second_half * cosine + first_half * sine_table,
        ],
        axis=-1,
    )


def rotary_back(grad_in, cosine, sine_table):
    half_width = grad_in.shape[-1] // 2
    first_half = grad_in[..., :half_width]
    second_half = grad_in[..., half_width:]
    return jnp.concatenate(
        [
            first_half * cosine + second_half * sine_table,
            second_half * cosine - first_half * sine_table,
        ],
        axis=-1,
    )


def rotary_tables(place_ids):
    freqs = ROPE_BASE ** (-(jnp.arange(HD // 2).astype(jnp.float32) * 2.0 / HD))
    angles = place_ids.astype(jnp.float32)[..., None] * freqs
    return (jnp.cos(angles), jnp.sin(angles))


def contract_rows(left, right):
    return lax.dot_general(
        left, right, (((0,), (0,)), ((), ())), preferred_element_type=jnp.float32
    )


def contract_cols(left, right):
    return lax.dot_general(
        left, right, (((1,), (1,)), ((), ())), preferred_element_type=jnp.float32
    )


def adam(master, moment_one, moment_two, grad_in, step_rate, decay_rate):
    first_new = BETA_ONE * moment_one + (1.0 - BETA_ONE) * grad_in
    second_new = BETA_TWO * moment_two + (1.0 - BETA_TWO) * grad_in * grad_in
    first_hat = first_new / (1.0 - BETA_ONE**STEP)
    second_hat = second_new / (1.0 - BETA_TWO**STEP)
    master_new = master - step_rate * (
        first_hat / (jnp.sqrt(second_hat) + ADAM_EPS) + decay_rate * master
    )
    return (master_new, first_new, second_new)


def body(
    tokens,
    output_grad,
    segment_ids,
    positions,
    qkv_weight,
    qkv_first,
    qkv_second,
    out_weight,
    out_first,
    out_second,
    gate_up_weight,
    gate_up_first,
    gate_up_second,
    down_weight,
    down_first,
    down_second,
    norm_gains,
    norm_first,
    norm_second,
    head_gains,
    head_first,
    head_second,
):
    n_ctx = lax.axis_size("ctx")
    ctx_rank = lax.axis_index("ctx")
    seq_count, local_len, width_model = tokens.shape
    seq_total = local_len * n_ctx
    group_size = H // KV
    scale_dot = 1.0 / math.sqrt(HD)

    def fetch_attention():
        return (
            lax.all_gather(qkv_weight.astype(jnp.bfloat16), ("dp", "ctx"), axis=0, tiled=True),
            lax.all_gather(out_weight.astype(jnp.bfloat16), ("dp", "ctx"), axis=0, tiled=True),
            lax.all_gather(
                norm_gains.astype(jnp.bfloat16), ("dp", "ctx"), axis=1, tiled=True
            ).astype(norm_gains.dtype),
        )

    def fetch_feed():
        return (
            lax.all_gather(gate_up_weight.astype(jnp.bfloat16), ("dp", "ctx"), axis=0, tiled=True),
            lax.all_gather(down_weight.astype(jnp.bfloat16), ("dp", "ctx"), axis=0, tiled=True),
        )

    inputs = tokens.astype(jnp.float32)
    qkv_full, out_full, norm_full = fetch_attention()
    normed, scale_one = rms_parts(inputs, norm_full[0])
    normed = normed.astype(jnp.bfloat16)
    projected = jnp.einsum("scd,de->sce", normed, qkv_full, preferred_element_type=jnp.float32)
    query_raw = projected[..., : H * HD].reshape(seq_count, local_len, KV, group_size, HD)
    keys_raw = projected[..., H * HD : (H + KV) * HD].reshape(seq_count, local_len, KV, HD)
    value_rows = (
        projected[..., (H + KV) * HD :].reshape(seq_count, local_len, KV, HD).astype(jnp.bfloat16)
    )
    cosine, sine_table = rotary_tables(positions)
    query_normed, query_scale = rms_parts(query_raw, head_gains[0])
    keys_normed, keys_scale = rms_parts(keys_raw, head_gains[1])
    query_rot = rotary(
        query_normed, cosine[:, :, None, None, :], sine_table[:, :, None, None, :]
    ).astype(jnp.bfloat16)
    keys_rot = rotary(keys_normed, cosine[:, :, None, :], sine_table[:, :, None, :]).astype(
        jnp.bfloat16
    )
    keys_all, values_all, segments_all = (
        lax.all_gather(keys_rot, "ctx", axis=1, tiled=True),
        lax.all_gather(value_rows, "ctx", axis=1, tiled=True),
        lax.all_gather(segment_ids, "ctx", axis=1, tiled=True),
    )
    key_item_rows = keys_all.transpose(0, 2, 1, 3).reshape(seq_count * KV, seq_total, HD)
    value_item_rows = values_all.transpose(0, 2, 1, 3).reshape(seq_count * KV, seq_total, HD)
    key_segments = jnp.repeat(segments_all, KV, axis=0)
    query_items = query_rot.transpose(0, 2, 3, 1, 4).reshape(
        seq_count * KV, group_size * local_len, HD
    )
    query_segments = jnp.repeat(segment_ids, KV, axis=0)
    query_index = ctx_rank * local_len + jnp.arange(local_len)
    causal = jnp.arange(seq_total)[None, :] <= query_index[:, None]

    def masked_scores(query_item, key_item, query_seg, key_seg):
        scores = contract_cols(query_item, key_item) * scale_dot
        allowed = causal & (query_seg[:, None] == key_seg[None, :])
        return jnp.where(allowed[None], scores.reshape(group_size, local_len, seq_total), -1e30)

    def attend(item_row):
        query_item, key_item, value_item, query_seg, key_seg = item_row
        scores = masked_scores(query_item, key_item, query_seg, key_seg)
        row_max = jnp.max(scores, axis=-1, keepdims=True)
        exp_scores = jnp.exp(scores - row_max)
        row_total = jnp.sum(exp_scores, axis=-1, keepdims=True)
        probs_low = (
            (exp_scores / row_total).astype(jnp.bfloat16).reshape(group_size * local_len, seq_total)
        )
        attended_item = jnp.dot(probs_low, value_item, preferred_element_type=jnp.float32)
        return (attended_item, (row_max + jnp.log(row_total))[..., 0])

    attended_items, log_total = lax.map(
        attend, (query_items, key_item_rows, value_item_rows, query_segments, key_segments)
    )
    attended = (
        attended_items.reshape(seq_count, KV, group_size, local_len, HD)
        .transpose(0, 3, 1, 2, 4)
        .reshape(seq_count, local_len, H * HD)
        .astype(jnp.bfloat16)
    )
    middle = inputs + jnp.einsum(
        "sch,hd->scd", attended, out_full, preferred_element_type=jnp.float32
    )
    feed_in, scale_two = rms_parts(middle, norm_full[1])
    feed_in = feed_in.astype(jnp.bfloat16)
    gate_up_full, down_full = fetch_feed()
    gate_up = jnp.einsum("scd,de->sce", feed_in, gate_up_full, preferred_element_type=jnp.float32)
    gate_part = gate_up[..., :FF]
    up_part = gate_up[..., FF:]
    sigmoid_gate = jax.nn.sigmoid(gate_part)
    silu_gate = gate_part * sigmoid_gate
    hidden = (silu_gate * up_part).astype(jnp.bfloat16)
    result = middle + jnp.einsum(
        "scf,fd->scd", hidden, down_full, preferred_element_type=jnp.float32
    )
    outputs = result.astype(jnp.bfloat16)
    gate_up_full, down_full = fetch_feed()
    qkv_full, out_full, norm_full = fetch_attention()
    grad_rows = output_grad.reshape(seq_count * local_len, width_model)
    hidden_rows = hidden.reshape(seq_count * local_len, FF)
    d_hidden = jnp.einsum("scd,fd->scf", output_grad, down_full, preferred_element_type=jnp.float32)
    down_grad = lax.psum_scatter(
        contract_rows(hidden_rows, grad_rows), ("dp", "ctx"), scatter_dimension=0, tiled=True
    )
    d_gate = d_hidden * up_part * sigmoid_gate * (1.0 + gate_part * (1.0 - sigmoid_gate))
    d_up = d_hidden * silu_gate
    d_gate_up = jnp.concatenate([d_gate, d_up], axis=-1).astype(jnp.bfloat16)
    feed_rows = feed_in.reshape(seq_count * local_len, width_model)
    d_gate_up_rows = d_gate_up.reshape(seq_count * local_len, 2 * FF)
    gate_up_grad = lax.psum_scatter(
        contract_rows(feed_rows, d_gate_up_rows), ("dp", "ctx"), scatter_dimension=0, tiled=True
    )
    d_feed = jnp.einsum("sce,de->scd", d_gate_up, gate_up_full, preferred_element_type=jnp.float32)
    d_middle_norm, gain_two_terms = norm_back(d_feed, middle, scale_two, norm_full[1])
    d_middle = output_grad.astype(jnp.float32) + d_middle_norm
    d_middle_low = d_middle.astype(jnp.bfloat16)
    out_grad_full = jnp.einsum(
        "sch,scd->hd", attended, d_middle_low, preferred_element_type=jnp.float32
    )
    d_attended = jnp.einsum(
        "scd,hd->sch", d_middle_low, out_full, preferred_element_type=jnp.float32
    ).astype(jnp.bfloat16)
    d_attended_items = (
        d_attended.reshape(seq_count, local_len, KV, group_size, HD)
        .transpose(0, 2, 3, 1, 4)
        .reshape(seq_count * KV, group_size * local_len, HD)
    )

    def attend_back(item_row):
        query_item, key_item, value_item, query_seg, key_seg, log_item, d_item = item_row
        scores = masked_scores(query_item, key_item, query_seg, key_seg)
        probs = jnp.exp(scores - log_item[..., None])
        probs_low = probs.astype(jnp.bfloat16).reshape(group_size * local_len, seq_total)
        d_probs = contract_cols(d_item, value_item).reshape(group_size, local_len, seq_total)
        inner = jnp.sum(probs * d_probs, axis=-1, keepdims=True)
        d_scores = (
            (probs * (d_probs - inner))
            .astype(jnp.bfloat16)
            .reshape(group_size * local_len, seq_total)
        )
        d_query_item = jnp.dot(d_scores, key_item, preferred_element_type=jnp.float32) * scale_dot
        d_key_item = contract_rows(d_scores, query_item) * scale_dot
        d_value_item = contract_rows(probs_low, d_item)
        return (d_query_item, d_key_item, d_value_item)

    d_query_items, d_key_items, d_value_items = lax.map(
        attend_back,
        (
            query_items,
            key_item_rows,
            value_item_rows,
            query_segments,
            key_segments,
            log_total,
            d_attended_items,
        ),
    )
    key_part, value_part = (
        lax.psum_scatter(
            d_key_items.reshape(seq_count, KV, seq_total, HD).astype(jnp.bfloat16),
            "ctx",
            scatter_dimension=2,
            tiled=True,
        ).astype(jnp.float32),
        lax.psum_scatter(
            d_value_items.reshape(seq_count, KV, seq_total, HD).astype(jnp.bfloat16),
            "ctx",
            scatter_dimension=2,
            tiled=True,
        ).astype(jnp.float32),
    )
    key_part = key_part.transpose(0, 2, 1, 3)
    value_part = value_part.transpose(0, 2, 1, 3)
    d_query_rot = d_query_items.reshape(seq_count, KV, group_size, local_len, HD).transpose(
        0, 3, 1, 2, 4
    )
    d_query_normed = rotary_back(
        d_query_rot, cosine[:, :, None, None, :], sine_table[:, :, None, None, :]
    )
    d_query, head_query_terms = norm_back(d_query_normed, query_raw, query_scale, head_gains[0])
    d_keys_normed = rotary_back(key_part, cosine[:, :, None, :], sine_table[:, :, None, :])
    d_keys, head_key_terms = norm_back(d_keys_normed, keys_raw, keys_scale, head_gains[1])
    d_projected = jnp.concatenate(
        [
            d_query.reshape(seq_count, local_len, H * HD),
            d_keys.reshape(seq_count, local_len, KV * HD),
            value_part.reshape(seq_count, local_len, KV * HD),
        ],
        axis=-1,
    ).astype(jnp.bfloat16)
    qkv_grad_full = jnp.einsum(
        "scd,sce->de", normed, d_projected, preferred_element_type=jnp.float32
    )
    d_normed = jnp.einsum("sce,de->scd", d_projected, qkv_full, preferred_element_type=jnp.float32)
    d_inputs, gain_one_terms = norm_back(d_normed, inputs, scale_one, norm_full[0])
    input_grad = (d_middle + d_inputs).astype(jnp.bfloat16)
    norm_terms = jnp.stack(
        [jnp.sum(gain_one_terms, axis=(0, 1)), jnp.sum(gain_two_terms, axis=(0, 1))]
    )
    qkv_grad, out_grad, norm_grad = (
        lax.psum_scatter(qkv_grad_full, ("dp", "ctx"), scatter_dimension=0, tiled=True),
        lax.psum_scatter(out_grad_full, ("dp", "ctx"), scatter_dimension=0, tiled=True),
        lax.psum_scatter(norm_terms, ("dp", "ctx"), scatter_dimension=1, tiled=True),
    )
    head_terms = jnp.stack(
        [jnp.sum(head_query_terms, axis=(0, 1, 2, 3)), jnp.sum(head_key_terms, axis=(0, 1, 2))]
    )
    head_grad = lax.psum(head_terms, ("dp", "ctx"))
    qkv_new = adam(qkv_weight, qkv_first, qkv_second, qkv_grad, RATE_QKV, DECAY)
    out_new = adam(out_weight, out_first, out_second, out_grad, RATE_OUT, DECAY)
    gate_up_new = adam(
        gate_up_weight, gate_up_first, gate_up_second, gate_up_grad, RATE_GATE_UP, DECAY
    )
    down_new = adam(down_weight, down_first, down_second, down_grad, RATE_DOWN, DECAY)
    norm_new = adam(norm_gains, norm_first, norm_second, norm_grad, RATE_GAIN, 0.0)
    head_new = adam(head_gains, head_first, head_second, head_grad, RATE_GAIN, 0.0)
    return (
        outputs,
        input_grad,
        qkv_new[0],
        qkv_new[1],
        qkv_new[2],
        out_new[0],
        out_new[1],
        out_new[2],
        gate_up_new[0],
        gate_up_new[1],
        gate_up_new[2],
        down_new[0],
        down_new[1],
        down_new[2],
        norm_new[0],
        norm_new[1],
        norm_new[2],
        head_new[0],
        head_new[1],
        head_new[2],
    )


def solution(mesh):
    in_specs = (
        P("dp", "ctx", None),
        P("dp", "ctx", None),
        P("dp", "ctx"),
        P("dp", "ctx"),
        P(("dp", "ctx"), None),
        P(("dp", "ctx"), None),
        P(("dp", "ctx"), None),
        P(("dp", "ctx"), None),
        P(("dp", "ctx"), None),
        P(("dp", "ctx"), None),
        P(("dp", "ctx"), None),
        P(("dp", "ctx"), None),
        P(("dp", "ctx"), None),
        P(("dp", "ctx"), None),
        P(("dp", "ctx"), None),
        P(("dp", "ctx"), None),
        P(None, ("dp", "ctx")),
        P(None, ("dp", "ctx")),
        P(None, ("dp", "ctx")),
        P(),
        P(),
        P(),
    )
    out_specs = (
        P("dp", "ctx", None),
        P("dp", "ctx", None),
        P(("dp", "ctx"), None),
        P(("dp", "ctx"), None),
        P(("dp", "ctx"), None),
        P(("dp", "ctx"), None),
        P(("dp", "ctx"), None),
        P(("dp", "ctx"), None),
        P(("dp", "ctx"), None),
        P(("dp", "ctx"), None),
        P(("dp", "ctx"), None),
        P(("dp", "ctx"), None),
        P(("dp", "ctx"), None),
        P(("dp", "ctx"), None),
        P(None, ("dp", "ctx")),
        P(None, ("dp", "ctx")),
        P(None, ("dp", "ctx")),
        P(),
        P(),
        P(),
    )
    return jax.shard_map(body, mesh=mesh, in_specs=in_specs, out_specs=out_specs, check_vma=False)
```

profile of v0, /device:TPU:0, one launch (start us, length us, event | category | flops | bytes accessed | tf_op | source)
XLA Modules:
  0.0 4453.3 jit_solution(1185946838953627720)
XLA Ops:
  9.9 43.2 all-gather
  57.1 53.4 %all-gather.8.cloned.1.call-done = bf16[2048,3072]{1,0:T(8,128)(2,1)} async-done(((bf16[64,3072]{1,0:T(8,128)(2,1)}), bf16[2048,3072]{1,0:T(8,128)(2,1)}) %all-gather.8.cloned.1.call-update) | async-done | bytes 12582928 | tf_op jit(solution)/shard_map/all_gather | solution.py:127
  182.1 38.7 all-gather.12.cloned.1.call-done
  220.8 196.4 %while.30 = (s32[]{:T(128)}, bf16[16,1024,64]{1,2,0:T(8,128)(2,1)S(1)}, f32[16,4,256]{2,1,0:T(4,128)}, s32[16,256]{1,0:T(8,128)S(1)}, s32[16,2048]{1,0:T(8,128)S...) while((s32[]{:T(128)}, ...), condition=%wide.region_6.7_spmd.clone.clone, body=%wide.region_3.6_spmd.clone.sunk.clone | while | flops 563608576 | bytes 37042288 | solution.py:191
  438.0 220.5 %all-gather.16.cloned.1.call-done = bf16[2048,16384]{1,0:T(8,128)(2,1)} async-done(((bf16[64,16384]{1,0:T(8,128)(2,1)}), bf16[2048,16384]{1,0:T(8,128)(2,1)}) %all-gather.16.cloned.1.call-update) | async-done | bytes 67108880 | tf_op jit(solution)/shard_map/all_gather | solution.py:136
  658.5 45.9 %fusion.50 = f32[2,256,16384]{2,1,0:T(8,128)} fusion(bf16[2048,16384]{1,0:T(8,128)(2,1)} %all-gather.16.cloned.1.call-done, f32[2,256,2048]{2,1,0:T(8,128)} %get-tuple-element.416, f32[2048]{0:T(1024)S(1)} %bitcast.318, f32[2,256]{1,0:T(2,128)S(1)} %add_rsqrt_fusion.2), kind=kOutput, calls=%fused_computation.70 | convolution fusion | flops 34362884096 | bytes 104867840 | tf_op jit(solution)/shard_map/scd,de->sce/dot_general | solution.py:206
  704.5 150.5 %all-gather.18.cloned.1.call-done = bf16[8192,2048]{1,0:T(8,128)(2,1)} async-done(((bf16[256,2048]{1,0:T(8,128)(2,1)}), bf16[8192,2048]{1,0:T(8,128)(2,1)}) %all-gather.18.cloned.1.call-update) | async-done | bytes 33554448 | tf_op jit(solution)/shard_map/all_gather | solution.py:137
  854.9 38.5 multiply_convert_fusion.2
  893.4 48.8 %multiply_reduce_fusion.2 = (f32[2048]{0:T(1024)}, f32[2,256]{1,0:T(2,128)S(1)}, f32[2,256,2048]{2,1,0:T(8,128)}) fusion(f32[2,256,2048]{2,1,0:T(8,128)} %get-tuple-element.416, f32[2,256]{1,0:T(2,128)S(1)} %add_rsqrt_fusion.2, f32[2048]{0:T(1024)S(1)} %bitcast.319, bf16[2048,16384]{1,0:T(8,128)(2,1)} %all-gather.16.cloned.1.call-done, ...), kind=kOutput, calls=%fused_computation.120 | convolution fusion | flops 34399584256 | bytes 92295168 | tf_op jit(solution)/shard_map/sce,de->scd/dot_general | solution.py:232
  964.6 663.6 %while.31 = (s32[]{:T(128)}, f32[16,1024,64]{1,2,0:T(8,128)}, bf16[16,2048,64]{1,2,0:T(8,128)(2,1)}, bf16[16,2048,64]{1,2,0:T(8,128)(2,1)}, s32[16,256]{1,0:T(8,...) while((s32[]{:T(128)}, f32[16,1024,64]{1,2,0:T(8,128)}, ...), condition=%wide.region_11.12_spmd.clone.clone, body=%wide.region_9.11_spmd.clone.sunk.clone | while | flops 1369115648 | bytes 76869808 | solution.py:265
  981.0 17.6 multiply_convert_fusion.12
  1022.6 17.6 multiply_convert_fusion.12
  1064.0 17.6 multiply_convert_fusion.12
  1105.5 17.6 multiply_convert_fusion.12
  1146.9 17.6 multiply_convert_fusion.12
  1188.4 17.6 multiply_convert_fusion.12
  1229.8 17.6 multiply_convert_fusion.12
  1271.3 17.6 multiply_convert_fusion.12
  1312.8 17.6 multiply_convert_fusion.12
  1354.3 17.6 multiply_convert_fusion.12
  1395.8 17.6 multiply_convert_fusion.12
  1437.2 17.6 multiply_convert_fusion.12
  1603.1 17.6 multiply_convert_fusion.12
  1678.6 48.4 %reduce-scatter.13.cloned.1.call-done = bf16[2,8,256,64]{2,3,1,0:T(8,128)(2,1)} async-done(((bf16[2,8,2048,64]{2,3,1,0:T(8,128)(2,1)}), bf16[2,8,256,64]{2,3,1,0:T(8,128)(2,1)}) %reduce-scatter.13.cloned.1.call-update) | async-done | bytes 524304 | tf_op jit(solution)/shard_map/reduce_scatter | solution.py:278
  1777.5 29.2 convolution_bitcast_fusion.3
  1807.5 56.2 %convolution_bitcast_fusion.2 = f32[2048,16384]{1,0:T(8,128)} fusion(bf16[2,256,8192]{2,1,0:T(8,128)(2,1)} %get-tuple-element.391, bf16[2,256,8192]{2,1,0:T(8,128)(2,1)} %get-tuple-element.390, f32[2,256,2048]{2,1,0:T(8,128)} %get-tuple-element.416, f32[2048]{0:T(1024)S(1)} %bitcast.321, f32[2,256]{1,0:T(2,128)S(1)} %copy-done.49), kind=kOutput, calls=%fused_computation.67 | convolution fusion | flops 34396438528 | bytes 155199488 | tf_op jit(solution)/shard_map/dot_general | solution.py:72
  1864.5 25.1 add_convert_fusion
  1889.7 40.5 psum.7
  1938.7 129.7 %reduce-scatter.19.cloned.1.call-done = f32[64,2048]{1,0:T(8,128)} async-done(((f32[2048,2048]{1,0:T(8,128)}), f32[64,2048]{1,0:T(8,128)}) %reduce-scatter.19.cloned.1.call-update) | async-done | bytes 524304 | tf_op jit(solution)/shard_map/reduce_scatter | solution.py:321
  2071.1 248.0 %reduce-scatter.17.cloned.1.call-done = f32[64,3072]{1,0:T(8,128)} async-done(((f32[2048,3072]{1,0:T(8,128)}), f32[64,3072]{1,0:T(8,128)}) %reduce-scatter.17.cloned.1.call-update) | async-done | bytes 786448 | tf_op jit(solution)/shard_map/reduce_scatter | solution.py:320
  2322.5 707.8 %reduce-scatter.21.cloned.1.call-done = f32[256,2048]{1,0:T(8,128)} async-done(((f32[8192,2048]{1,0:T(8,128)}), f32[256,2048]{1,0:T(8,128)}) %reduce-scatter.21.cloned.1.call-update) | async-done | bytes 2097168 | tf_op jit(solution)/shard_map/reduce_scatter | solution.py:221
  3037.2 1398.0 %reduce-scatter.25.cloned.1.call-done = f32[64,16384]{1,0:T(8,128)} async-done(((f32[2048,16384]{1,0:T(8,128)}), f32[64,16384]{1,0:T(8,128)}) %reduce-scatter.25.cloned.1.call-update) | async-done | bytes 4194320
  (628 shorter events, 886.4 us)
Async XLA Ops:
  7.2 103.4 %all-gather.8.cloned.1.call-start = ((), (), s32[]{:S(2)}) async-start(), calls=%async_computation.7 | async-start | bytes 12976128 | tf_op jit(solution)/shard_map/all_gather | solution.py:127
  9.2 164.3 %all-gather.10.cloned.1.call-start = ((), (), s32[]{:S(2)}) async-start(), calls=%async_computation.8 | async-start | bytes 4718592 | tf_op jit(solution)/shard_map/all_gather | solution.py:160
  54.6 69.3 %copy-start.46 = (f32[64]{0:T(128)}, f32[64]{0:T(128)S(1)}, u32[]{:S(2)}) copy-start(f32[64]{0:T(128)S(1)} %get-tuple-element.413) | copy-start | bytes 772
  54.6 108.4 %copy-start.42 = (f32[64]{0:T(128)}, f32[64]{0:T(128)S(1)}, u32[]{:S(2)}) copy-start(f32[64]{0:T(128)S(1)} %get-tuple-element.414) | copy-start | bytes 772
  56.7 63.9 %copy-start.39 = (f32[2,256]{1,0:T(2,128)}, f32[2,256]{1,0:T(2,128)S(1)}, u32[]{:S(2)}) copy-start(f32[2,256]{1,0:T(2,128)S(1)} %add_rsqrt_fusion.3) | copy-start | bytes 6148
  57.1 107.4 %copy-start.19 = (f32[2,256,32]{1,2,0:T(8,128)}, f32[2,256,32]{1,2,0:T(8,128)S(1)}, u32[]{:S(2)}) copy-start(f32[2,256,32]{1,2,0:T(8,128)S(1)} %get-tuple-element.411) | copy-start | bytes 196612
  57.1 107.4 %copy-start.21 = (f32[2,256,32]{1,2,0:T(8,128)}, f32[2,256,32]{1,2,0:T(8,128)S(1)}, u32[]{:S(2)}) copy-start(f32[2,256,32]{1,2,0:T(8,128)S(1)} %get-tuple-element.412) | copy-start | bytes 196612
  57.1 63.5 %copy-start.33 = (f32[1,2048]{1,0:T(1,128)}, f32[1,2048]{1,0:T(1,128)S(1)}, u32[]{:S(2)}) copy-start(f32[1,2048]{1,0:T(1,128)S(1)} %get-tuple-element.410) | copy-start | bytes 24580
  57.1 885.2 %copy-start.36 = (f32[1,2048]{1,0:T(1,128)}, f32[1,2048]{1,0:T(1,128)S(1)}, u32[]{:S(2)}) copy-start(f32[1,2048]{1,0:T(1,128)S(1)} %get-tuple-element.409) | copy-start | bytes 24580
  125.6 95.2 %all-gather.12.cloned.1.call-start = ((), (), s32[]{:S(2)}) async-start(), calls=%async_computation.9 | async-start | bytes 4718592 | tf_op jit(solution)/shard_map/all_gather | solution.py:161
  127.9 299.1 %all-gather.14.cloned.1.call-start = ((), (), s32[]{:S(2)}) async-start(), calls=%async_computation.10 | async-start | bytes 8650752 | tf_op jit(solution)/shard_map/all_gather | solution.py:128
  128.8 529.7 %all-gather.16.cloned.1.call-start = ((), (), s32[]{:S(2)}) async-start(), calls=%async_computation.11 | async-start | bytes 69206016 | tf_op jit(solution)/shard_map/all_gather | solution.py:136
  132.9 722.1 %all-gather.18.cloned.1.call-start = ((), (), s32[]{:S(2)}) async-start(), calls=%async_computation.12 | async-start | bytes 34603008 | tf_op jit(solution)/shard_map/all_gather | solution.py:137
  134.1 1542.5 %reduce-scatter.15.cloned.1.call-start = ((), (), s32[]{:S(2)}) async-start(), calls=%async_computation.14 | async-start | bytes 4718592 | tf_op jit(solution)/shard_map/reduce_scatter | solution.py:284
  438.0 504.3 %copy-start.48 = (f32[2,256]{1,0:T(2,128)}, f32[2,256]{1,0:T(2,128)S(1)}, u32[]{:S(2)}) copy-start(f32[2,256]{1,0:T(2,128)S(1)} %add_rsqrt_fusion.2) | copy-start | bytes 6148
  658.5 196.4 %copy-start.17 = (bf16[2,256,2048]{2,1,0:T(8,128)(2,1)S(1)}, bf16[2,256,2048]{2,1,0:T(8,128)(2,1)}, u32[]{:S(2)}) copy-start(bf16[2,256,2048]{2,1,0:T(8,128)(2,1)} %param.27) | copy-start | bytes 6291460
  1628.2 98.9 %reduce-scatter.13.cloned.1.call-start = ((), (), s32[]{:S(2)}) async-start(), calls=%async_computation.13 | async-start | bytes 4718592 | tf_op jit(solution)/shard_map/reduce_scatter | solution.py:278
  1628.9 308.2 %reduce-scatter.23.cloned.1.call-start = ((), (), s32[]{:S(2)}) async-start(), calls=%async_computation.18 | async-start | bytes 1081344
  1748.9 319.4 %reduce-scatter.19.cloned.1.call-start = ((), (), s32[]{:S(2)}) async-start(), calls=%async_computation.16 | async-start | bytes 17301504 | tf_op jit(solution)/shard_map/reduce_scatter | solution.py:321
  1762.4 556.8 %reduce-scatter.17.cloned.1.call-start = ((), (), s32[]{:S(2)}) async-start(), calls=%async_computation.15 | async-start | bytes 25952256 | tf_op jit(solution)/shard_map/reduce_scatter | solution.py:320
  1775.9 1254.4 %reduce-scatter.21.cloned.1.call-start = ((), (), s32[]{:S(2)}) async-start(), calls=%async_computation.17 | async-start | bytes 69206016 | tf_op jit(solution)/shard_map/reduce_scatter | solution.py:221
  1806.8 2628.4 %reduce-scatter.25.cloned.1.call-start = ((), (), s32[]{:S(2)}) async-start(), calls=%async_computation.19 | async-start | bytes 138412032
  1864.4 65.8 %copy-start.51 = (f32[2,256]{1,0:T(2,128)S(1)}, f32[2,256]{1,0:T(2,128)}, u32[]{:S(2)}) copy-start(f32[2,256]{1,0:T(2,128)} %get-tuple-element.323) | copy-start | bytes 6148
  1864.5 65.8 %copy-start.50 = (f32[2,64]{1,0:T(2,128)S(1)}, f32[2,64]{1,0:T(2,128)}, u32[]{:S(2)}) copy-start(f32[2,64]{1,0:T(2,128)} %param.45) | copy-start | bytes 1540
  1864.5 65.8 %copy-start.52 = (f32[2,64]{1,0:T(2,128)S(1)}, f32[2,64]{1,0:T(2,128)}, u32[]{:S(2)}) copy-start(f32[2,64]{1,0:T(2,128)} %param.46) | copy-start | bytes 1540
  1864.5 65.8 %copy-start.53 = (f32[2,64]{1,0:T(2,128)S(1)}, f32[2,64]{1,0:T(2,128)}, u32[]{:S(2)}) copy-start(f32[2,64]{1,0:T(2,128)} %param.47) | copy-start | bytes 1540
  1864.5 66.4 %copy-start.9 = (bf16[2,256,2048]{2,1,0:T(8,128)(2,1)S(1)}, bf16[2,256,2048]{2,1,0:T(8,128)(2,1)}, u32[]{:S(2)}) copy-start(bf16[2,256,2048]{2,1,0:T(8,128)(2,1)} %param.26) | copy-start | bytes 6291460
  1864.5 66.4 %copy-start.35 = (f32[1,2048]{1,0:T(1,128)S(1)}, f32[1,2048]{1,0:T(1,128)}, u32[]{:S(2)}) copy-start(f32[1,2048]{1,0:T(1,128)} %copy-done.33) | copy-start | bytes 24580
  1864.5 66.4 %copy-start.41 = (f32[2,256]{1,0:T(2,128)S(1)}, f32[2,256]{1,0:T(2,128)}, u32[]{:S(2)}) copy-start(f32[2,256]{1,0:T(2,128)} %copy-done.39) | copy-start | bytes 6148
  1931.0 137.4 %copy-start.16 = (f32[64,2048]{1,0:T(8,128)S(1)}, f32[64,2048]{1,0:T(8,128)}, u32[]{:S(2)}) copy-start(f32[64,2048]{1,0:T(8,128)} %param.33) | copy-start | bytes 1572868
  1937.2 382.0 %copy-start.14 = (f32[64,3072]{1,0:T(8,128)S(1)}, f32[64,3072]{1,0:T(8,128)}, u32[]{:S(2)}) copy-start(f32[64,3072]{1,0:T(8,128)} %param.30) | copy-start | bytes 2359300
  1938.7 1091.6 %copy-start.11 = (f32[256,2048]{1,0:T(8,128)S(1)}, f32[256,2048]{1,0:T(8,128)}, u32[]{:S(2)}) copy-start(f32[256,2048]{1,0:T(8,128)} %param.39) | copy-start | bytes 6291460
  (54 other events, 311.1 us)
Sparse Core Ops, SparseCore 0:
  11.6 98.9 all-gather.7
  125.7 47.7 all-gather.9
  175.7 45.0 all-gather.11
  224.2 75.8 all-gather.13
  303.5 354.9 all-gather.15
  661.9 192.9 all-gather.17
  1628.3 48.2 reduce-scatter.14
  1678.8 48.1 reduce-scatter.12
  1749.1 132.9 reduce-scatter.22
  1884.3 183.9 reduce-scatter.18
  2075.9 243.1 reduce-scatter.16
  2321.3 708.9 reduce-scatter.20
  3032.7 1402.4 reduce-scatter.24
where the time goes:
time: 4460 us; the launch traced here: 4450 us
  waiting for transfers between devices  3000 us (67%)
  matrix products  730 us (16%)
  other arithmetic  466 us (10%)
  local copies, waits for them, and re-layouts  140 us (3%)
  blocking collectives  97.9 us (2%)
    unnamed x15, waiting for transfers between devices  1400 us
    reduce_scatter x1, waiting for transfers between devices, body(): lax.psum_scatter(contract_rows(hidden_rows, grad_rows), ('dp', 'ctx'), sc...  708 us
    sub x16, other arithmetic, attend_back(): d_probs - inner  281 us
    dot_general x48, matrix products, contract_cols(): lax.dot_general(left, right, (((1,), (1,)), ((), ())), preferred_element_...  263 us
    reduce_scatter x1, waiting for transfers between devices, body(): lax.psum_scatter(qkv_grad_full, ('dp', 'ctx'), scatter_dimension=0, tiled...  248 us
    all_gather x1, waiting for transfers between devices, fetch_feed(): lax.all_gather(gate_up_weight.astype(jnp.bfloat16), ('dp', 'ctx'), axis=0...  221 us
    dot_general x34, matrix products, contract_rows(): lax.dot_general(left, right, (((0,), (0,)), ((), ())), preferred_element_...  154 us
    all_gather x1, waiting for transfers between devices, fetch_feed(): lax.all_gather(down_weight.astype(jnp.bfloat16), ('dp', 'ctx'), axis=0, t...  150 us
  transfers between devices with their start and end apart: 13, of which 11 were waited for; matrix products, arithmetic and copies ran while one was open for 11% of the time, Pallas kernels for 0%

commit v1 on v0

v1 whole, which is shorter than its diff:
```python
import functools
import math

import jax
import jax.numpy as jnp
from jax import lax
from jax.experimental import pallas as pl
from jax.experimental.pallas import tpu as pltpu
from jax.sharding import PartitionSpec as P

H = 32
KV = 8
HD = 64
G = H // KV
STEP = 5

EPS = 1e-05
ROPE_BASE = 1000000.0
BETA_ONE = 0.9
BETA_TWO = 0.95
ADAM_EPS = 1e-08
DECAY = 0.1
RATE_QKV = 0.05
RATE_OUT = 0.3
RATE_GATE_UP = 0.05
RATE_DOWN = 0.03
RATE_GAIN = 0.5

LOW = jnp.bfloat16
F32 = jnp.float32


def rms_scale(values):
    return lax.rsqrt(jnp.mean(values * values, axis=-1, keepdims=True) + EPS)


def norm_back(scaled, values, inv_rms):
    inner = jnp.mean(scaled * values, axis=-1, keepdims=True)
    return inv_rms * (scaled - values * inv_rms * inv_rms * inner)


def rotary(values, cosine, sine):
    first, second = values[..., : HD // 2], values[..., HD // 2 :]
    return jnp.concatenate([first * cosine - second * sine, second * cosine + first * sine], axis=-1)


def rotary_back(grad, cosine, sine):
    first, second = grad[..., : HD // 2], grad[..., HD // 2 :]
    return jnp.concatenate([first * cosine + second * sine, second * cosine - first * sine], axis=-1)


def rotary_tables(place_ids):
    freqs = ROPE_BASE ** (-(jnp.arange(HD // 2).astype(F32) * 2.0 / HD))
    angles = place_ids.astype(F32)[..., None] * freqs
    return (jnp.cos(angles), jnp.sin(angles))


def dot(left, right, dims):
    return lax.dot_general(left, right, (dims, ((), ())), preferred_element_type=F32)


NN = ((1,), (0,))
NT = ((1,), (1,))
TN = ((0,), (0,))


def adam(master, moment_one, moment_two, grad, step_rate, decay_rate):
    first_new = BETA_ONE * moment_one + (1.0 - BETA_ONE) * grad
    second_new = BETA_TWO * moment_two + (1.0 - BETA_TWO) * grad * grad
    first_hat = first_new / (1.0 - BETA_ONE**STEP)
    second_hat = second_new / (1.0 - BETA_TWO**STEP)
    master_new = master - step_rate * (
        first_hat / (jnp.sqrt(second_hat) + ADAM_EPS) + decay_rate * master
    )
    return (master_new, first_new, second_new)


def chunk_mask(chunk, length, start, query_index):
    key_index = chunk * length + lax.broadcasted_iota(jnp.int32, (length, start.shape[1]), 0)
    return (key_index >= start) & (key_index <= query_index)


def for_chunks(meta_ref, step):
    place, low, full = meta_ref[0], meta_ref[1], meta_ref[2]

    @pl.loop(low, full)
    def _(chunk):
        step(chunk, True)

    @pl.loop(full, place)
    def _(chunk):
        step(chunk, False)

    step(place, True)


def attend_kernel(turned, meta_ref, start_ref, index_ref, query_ref, kv_ref, out_ref, log_ref, acc_ref):
    length = query_ref.shape[1] // G
    start, query_index = start_ref[...], index_ref[...]
    lane = lax.broadcasted_iota(jnp.int32, (length, 2 * HD), 1)
    acc_ref[...] = jnp.zeros_like(acc_ref)

    def step(chunk, masked):
        slot = kv_ref.shape[0] - 1 - chunk if turned else chunk
        kv = kv_ref[slot, 0]
        ones_v = jnp.where(lane < HD, jnp.ones_like(kv), kv)
        probs = jnp.exp(dot(kv, query_ref[0], NT))
        if masked:
            probs = jnp.where(chunk_mask(chunk, length, start, query_index), probs, 0.0)
        acc_ref[...] += dot(ones_v, probs.astype(LOW), TN)

    for_chunks(meta_ref, step)
    total = acc_ref[:1, :]
    log_ref[0] = jnp.log(total)
    mixed = acc_ref[HD:, :] / total
    rows = [mixed[:, head * length : (head + 1) * length] for head in range(G)]
    out_ref[...] = jnp.concatenate(rows, axis=0).T.astype(out_ref.dtype)


def attend_back_kernel(
    turned,
    meta_ref,
    start_ref,
    index_ref,
    query_ref,
    kv_ref,
    grad_ref,
    log_ref,
    inner_ref,
    dq_ref,
    dkv_ref,
    acc_ref,
):
    length = query_ref.shape[1] // G
    start, query_index = start_ref[...], index_ref[...]
    acc_ref[...] = jnp.zeros_like(acc_ref)
    dkv_ref[...] = jnp.zeros_like(dkv_ref)

    def step(chunk, masked):
        slot = kv_ref.shape[0] - 1 - chunk if turned else chunk
        kv = kv_ref[slot, 0]
        total = jnp.zeros((length, 2 * HD), F32)
        for head in range(G):
            part = pl.ds(head * length, length)
            query, grad = query_ref[0, part], grad_ref[0, part]
            probs = jnp.exp(dot(kv, query, NT) - log_ref[0, :, part])
            if masked:
                mask = chunk_mask(chunk, length, start[:, :length], query_index[:, :length])
                probs = jnp.where(mask, probs, 0.0)
            d_probs = dot(kv, grad, NT)
            d_scores = (probs * (d_probs - inner_ref[0, :, part])).astype(LOW)
            total = total + dot(d_scores, query, NN) + dot(probs.astype(LOW), grad, NN)
            acc_ref[:, part] += dot(kv, d_scores, TN)
        dkv_ref[slot, 0] = total.astype(dkv_ref.dtype)

    for_chunks(meta_ref, step)
    rows = [acc_ref[:HD, head * length : (head + 1) * length] for head in range(G)]
    dq_ref[...] = jnp.concatenate(rows, axis=0).T * (1.0 / math.sqrt(HD))


def attention_specs(n_ctx, length):
    query = pl.BlockSpec((1, G * length, 2 * HD), lambda h, *_: (h, 0, 0))
    kv = pl.BlockSpec((n_ctx, 1, length, 2 * HD), lambda h, *_: (0, h, 0, 0))
    row = pl.BlockSpec((1, 1, G * length), lambda h, *_: (h, 0, 0))
    start = pl.BlockSpec((1, G * length), lambda h, *_: (0, 0))
    natural = pl.BlockSpec((length, G * HD), lambda h, *_: (0, h))
    return query, kv, row, start, natural


def attend(turned, meta, start, index, query, kv_all):
    n_ctx, heads, length, _ = kv_all.shape
    q_spec, kv_spec, row_spec, start_spec, natural = attention_specs(n_ctx, length)
    pairs = heads * G * length * n_ctx * length
    return pl.pallas_call(
        functools.partial(attend_kernel, turned),
        grid_spec=pltpu.PrefetchScalarGridSpec(
            num_scalar_prefetch=1,
            grid=(heads,),
            in_specs=[start_spec, start_spec, q_spec, kv_spec],
            out_specs=[natural, row_spec],
            scratch_shapes=[pltpu.VMEM((2 * HD, G * length), F32)],
        ),
        out_shape=[
            jax.ShapeDtypeStruct((length, heads * G * HD), LOW),
            jax.ShapeDtypeStruct((heads, 1, G * length), F32),
        ],
        compiler_params=pltpu.CompilerParams(vmem_limit_bytes=40 * 2**20),
        cost_estimate=pl.CostEstimate(
            flops=pairs * 512, bytes_accessed=16 * 2**20, transcendentals=pairs
        ),
        name="attend",
    )(meta, start, index, query, kv_all)


def attend_back(turned, meta, start, index, query, kv_all, grad, log_total, inner):
    n_ctx, heads, length, _ = kv_all.shape
    q_spec, kv_spec, row_spec, start_spec, natural = attention_specs(n_ctx, length)
    pairs = heads * G * length * n_ctx * length
    return pl.pallas_call(
        functools.partial(attend_back_kernel, turned),
        grid_spec=pltpu.PrefetchScalarGridSpec(
            num_scalar_prefetch=1,
            grid=(heads,),
            in_specs=[start_spec, start_spec, q_spec, kv_spec, q_spec, row_spec, row_spec],
            out_specs=[natural, kv_spec],
            scratch_shapes=[pltpu.VMEM((2 * HD, G * length), F32)],
        ),
        out_shape=[
            jax.ShapeDtypeStruct((length, heads * G * HD), F32),
            jax.ShapeDtypeStruct(kv_all.shape, LOW),
        ],
        compiler_params=pltpu.CompilerParams(vmem_limit_bytes=40 * 2**20),
        cost_estimate=pl.CostEstimate(
            flops=pairs * 1280, bytes_accessed=32 * 2**20, transcendentals=pairs
        ),
        name="attend_back",
    )(meta, start, index, query, kv_all, grad, log_total, inner)


def partners(values, axis, shift):
    count = lax.axis_size(axis)
    return lax.ppermute(values, axis, [(i, i ^ shift) for i in range(count)])


def gather_dp(values):
    count = lax.axis_size("dp")
    return [values] + [partners(values, "dp", shift) for shift in range(1, count)]


def reduce_dp(blocks):
    total = blocks[0].astype(F32)
    for shift in range(1, len(blocks)):
        total = total + partners(blocks[shift].astype(LOW), "dp", shift).astype(F32)
    return total


def exchange(blocks, axis):
    count = blocks.shape[0]
    rank = lax.axis_index(axis)
    own = lax.dynamic_index_in_dim(blocks, rank, 0, keepdims=True)
    result = lax.dynamic_update_slice_in_dim(jnp.zeros_like(blocks), own, rank, 0)
    for shift in range(1, count):
        block = lax.dynamic_index_in_dim(blocks, rank ^ shift, 0, keepdims=True)
        block = partners(block, axis, shift)
        result = lax.dynamic_update_slice_in_dim(result, block, rank ^ shift, 0)
    return result


def mirror(values):
    count = lax.axis_size("ctx")
    return lax.ppermute(values, "ctx", [(i, count - 1 - i) for i in range(count)])


def body(
    tokens,
    output_grad,
    segment_ids,
    positions,
    qkv_weight,
    qkv_first,
    qkv_second,
    out_weight,
    out_first,
    out_second,
    gate_up_weight,
    gate_up_first,
    gate_up_second,
    down_weight,
    down_first,
    down_second,
    norm_gains,
    norm_first,
    norm_second,
    head_gains,
    head_first,
    head_second,
):
    n_dp, n_ctx = lax.axis_size("dp"), lax.axis_size("ctx")
    ctx_rank = lax.axis_index("ctx")
    seqs, length, width = tokens.shape
    own = norm_gains.shape[1]
    ff = down_weight.shape[0] * n_dp * n_ctx
    part = ff // n_dp
    everyone = ("dp", "ctx")

    gain_one, gain_two = norm_gains[0][:, None], norm_gains[1][:, None]
    qkv_low = qkv_weight.astype(LOW).astype(F32)
    gate_up_low = gate_up_weight.astype(LOW).astype(F32)
    qkv_full = lax.all_gather((qkv_low * gain_one).astype(LOW), everyone, axis=0, tiled=True)
    gate_up_blocks = (
        (gate_up_low * gain_two).astype(LOW).reshape(own, 2, n_dp, part).transpose(2, 0, 1, 3)
    )
    gate_up_mine = exchange(gate_up_blocks.reshape(n_dp, own, 2 * part), "dp")
    gate_up_part = lax.all_gather(
        gate_up_mine.reshape(n_dp * own, 2 * part), "ctx", axis=0, tiled=True
    )
    down_part = lax.all_gather(down_weight.astype(LOW), "ctx", axis=0, tiled=True)
    out_full = lax.all_gather(out_weight.astype(LOW), everyone, axis=0, tiled=True)

    places = jnp.stack([segment_ids, positions], axis=1)
    tokens_of, grads_of, places_of, rank_of = [], [], [], []
    for seq in range(seqs):
        turned = seq % 2 == 1
        tokens_of.append(mirror(tokens[seq]) if turned else tokens[seq])
        grads_of.append(mirror(output_grad[seq]) if turned else output_grad[seq])
        places_of.append(mirror(places[seq]) if turned else places[seq])
        rank_of.append(n_ctx - 1 - ctx_rank if turned else ctx_rank)

    def project(seq):
        inputs = tokens_of[seq].astype(F32)
        scale_one = rms_scale(inputs)
        normed = (inputs * scale_one).astype(LOW)
        projected = dot(normed, qkv_full, NN)
        query_raw = projected[:, : H * HD].reshape(length, H, HD)
        keys_raw = projected[:, H * HD : (H + KV) * HD].reshape(length, KV, HD)
        values = projected[:, (H + KV) * HD :].reshape(length, KV, HD).astype(LOW)
        cosine, sine = rotary_tables(places_of[seq][1])
        cosine, sine = cosine[:, None, :], sine[:, None, :]
        query_scale, keys_scale = rms_scale(query_raw), rms_scale(keys_raw)
        query_rot = rotary(query_raw * query_scale * head_gains[0], cosine, sine).astype(LOW)
        keys_rot = rotary(keys_raw * keys_scale * head_gains[1], cosine, sine).astype(LOW)
        kv = jnp.concatenate([keys_rot, values], axis=-1).transpose(1, 0, 2)
        kv_all = lax.all_gather(kv, "ctx", axis=0)
        query = query_rot * LOW(1.0 / math.sqrt(HD))
        query = query.reshape(length, KV, G, HD).transpose(1, 2, 0, 3)
        query = jnp.pad(query, ((0, 0),) * 3 + ((0, HD),)).reshape(KV, G * length, 2 * HD)
        index = rank_of[seq] * length + jnp.arange(length, dtype=jnp.int32)
        start = jnp.where(places_of[seq][0] == 0, 0, index - places_of[seq][1])
        full = jnp.minimum((jnp.max(start) + length - 1) // length, rank_of[seq])
        low = jnp.minimum(jnp.min(start) // length, full)
        meta = jnp.stack([rank_of[seq], low, full]).astype(jnp.int32)
        start = jnp.tile(start[None, :], (1, G))
        index = jnp.tile(index[None, :], (1, G))
        keep = (inputs, scale_one, normed, query_raw, keys_raw, query_scale, keys_scale)
        return keep + (cosine, sine), (meta, start, index, query, kv_all)

    def feed(seq, keep, attended):
        middle = keep[0] + dot(attended, out_full, NN)
        scale_two = rms_scale(middle)
        feed_in = (middle * scale_two).astype(LOW)
        feed_in = feed_in.reshape(length, n_dp, n_ctx, own).transpose(0, 2, 1, 3)
        feed_all = jnp.concatenate(gather_dp(feed_in.reshape(length, width)), axis=0)
        return middle, scale_two, feed_all

    def hidden_units(seq, feed_all, grad_all):
        gate = dot(feed_all, gate_up_part[:, :part], NN)
        up = dot(feed_all, gate_up_part[:, part:], NN)
        sigmoid_gate = jax.nn.sigmoid(gate)
        silu_gate = gate * sigmoid_gate
        hidden = (silu_gate * up).astype(LOW)
        d_hidden = dot(grad_all, down_part, NT)
        d_gate = d_hidden * up * sigmoid_gate * (1.0 + gate * (1.0 - sigmoid_gate))
        d_up = d_hidden * silu_gate
        d_gate_up = jnp.concatenate([d_gate.astype(LOW), d_up.astype(LOW)], axis=1)
        d_feed = reduce_dp(jnp.split(dot(d_gate_up, gate_up_part, NT).astype(LOW), n_dp))
        result = reduce_dp(jnp.split(dot(hidden, down_part, NN).astype(LOW), n_dp))
        d_feed = d_feed.reshape(length, n_ctx, n_dp, own).transpose(0, 2, 1, 3)
        return hidden, d_gate_up, d_feed.reshape(length, width), result

    def attention_grad(seq, middle, scale_two, d_feed, attended):
        d_middle = grads_of[seq].astype(F32) + norm_back(d_feed, middle, scale_two)
        d_middle_low = d_middle.astype(LOW)
        d_attended = dot(d_middle_low, out_full, NT).astype(LOW)
        inner = (
            jnp.sum(
                (d_attended.astype(F32) * attended.astype(F32)).reshape(length, KV, G, HD), axis=-1
            )
            .transpose(1, 2, 0)
            .reshape(KV, 1, G * length)
        )
        grad_items = d_attended.reshape(length, KV, G, HD).transpose(1, 2, 0, 3)
        grad_items = jnp.pad(grad_items, ((0, 0),) * 3 + ((HD, 0),))
        return d_middle, d_middle_low, grad_items.reshape(KV, G * length, 2 * HD), inner

    def project_back(seq, keep, d_query_rot, d_kv):
        inputs, scale_one, normed, query_raw, keys_raw, query_scale, keys_scale, cosine, sine = keep
        d_kv = lax.psum_scatter(d_kv, "ctx", scatter_dimension=0, tiled=False)
        d_kv = d_kv.transpose(1, 0, 2).astype(F32)
        d_query_norm = rotary_back(d_query_rot.reshape(length, H, HD), cosine, sine)
        d_query = norm_back(d_query_norm * head_gains[0], query_raw, query_scale)
        d_keys_norm = rotary_back(d_kv[..., :HD], cosine, sine)
        d_keys = norm_back(d_keys_norm * head_gains[1], keys_raw, keys_scale)
        d_projected = jnp.concatenate(
            [
                d_query.astype(LOW).reshape(length, H * HD),
                d_keys.astype(LOW).reshape(length, KV * HD),
                d_kv[..., HD:].astype(LOW).reshape(length, KV * HD),
            ],
            axis=1,
        )
        head_terms = jnp.stack(
            [
                jnp.sum(d_query_norm * query_raw * query_scale, axis=(0, 1)),
                jnp.sum(d_keys_norm * keys_raw * keys_scale, axis=(0, 1)),
            ]
        )
        d_inputs = norm_back(dot(d_projected, qkv_full, NT), inputs, scale_one)
        return d_projected, head_terms, d_inputs

    each = range(seqs)
    grad_alls = [jnp.concatenate(gather_dp(grads_of[seq]), axis=0) for seq in each]
    keeps, items = zip(*[project(seq) for seq in each])
    attendeds, logs = zip(*[attend(seq % 2 == 1, *items[seq]) for seq in each])
    middles, scales, feed_alls = zip(*[feed(seq, keeps[seq], attendeds[seq]) for seq in each])
    hiddens, d_gate_ups, d_feeds, results = zip(
        *[hidden_units(seq, feed_alls[seq], grad_alls[seq]) for seq in each]
    )
    outputs = [(middles[seq] + results[seq]).astype(LOW) for seq in each]
    gate_up_sum = sum(dot(feed_alls[seq], d_gate_ups[seq], TN) for seq in each).astype(LOW)
    gate_up_grad = lax.psum_scatter(gate_up_sum, "ctx", scatter_dimension=0, tiled=True)
    gate_up_grad = exchange(gate_up_grad.reshape(n_dp, own, 2 * part), "dp")
    gate_up_grad = (
        gate_up_grad.reshape(n_dp, own, 2, part).transpose(1, 2, 0, 3).reshape(own, 2 * ff)
    ).astype(F32)
    down_sum = sum(dot(hiddens[seq], grad_alls[seq], TN) for seq in each).astype(LOW)
    down_grad = lax.psum_scatter(down_sum, "ctx", scatter_dimension=0, tiled=True).astype(F32)

    d_middles, d_middle_lows, grad_items, inners = zip(
        *[attention_grad(s, middles[s], scales[s], d_feeds[s], attendeds[s]) for s in each]
    )
    d_queries, d_kvs = zip(
        *[attend_back(s % 2 == 1, *items[s], grad_items[s], logs[s], inners[s]) for s in each]
    )
    d_projecteds, head_terms, d_inputs = zip(
        *[project_back(s, keeps[s], d_queries[s], d_kvs[s]) for s in each]
    )
    head_grad = lax.psum(sum(head_terms), everyone)
    input_grads = [(d_middles[s] + d_inputs[s]).astype(LOW) for s in each]
    attention_sum = jnp.concatenate(
        [
            sum(dot(keeps[s][2], d_projecteds[s], TN) for s in each).astype(LOW),
            sum(dot(attendeds[s], d_middle_lows[s], TN) for s in each).astype(LOW),
        ],
        axis=1,
    )
    attention_weight_grad = lax.psum_scatter(
        attention_sum, everyone, scatter_dimension=0, tiled=True
    ).astype(F32)
    qkv_grad = attention_weight_grad[:, : qkv_weight.shape[1]]
    out_grad = attention_weight_grad[:, qkv_weight.shape[1] :]

    def placed(values):
        return jnp.stack([mirror(values[s]) if s % 2 == 1 else values[s] for s in each])

    norm_grad = jnp.stack(
        [jnp.sum(qkv_low * qkv_grad, axis=1), jnp.sum(gate_up_low * gate_up_grad, axis=1)]
    )
    qkv_new = adam(qkv_weight, qkv_first, qkv_second, qkv_grad * gain_one, RATE_QKV, DECAY)
    out_new = adam(out_weight, out_first, out_second, out_grad, RATE_OUT, DECAY)
    gate_up_new = adam(
        gate_up_weight,
        gate_up_first,
        gate_up_second,
        gate_up_grad * gain_two,
        RATE_GATE_UP,
        DECAY,
    )
    down_new = adam(down_weight, down_first, down_second, down_grad, RATE_DOWN, DECAY)
    norm_new = adam(norm_gains, norm_first, norm_second, norm_grad, RATE_GAIN, 0.0)
    head_new = adam(head_gains, head_first, head_second, head_grad, RATE_GAIN, 0.0)
    return (
        placed(outputs),
        placed(input_grads),
        *qkv_new,
        *out_new,
        *gate_up_new,
        *down_new,
        *norm_new,
        *head_new,
    )


def solution(mesh):
    tokens_spec = P("dp", "ctx", None)
    matrix = P(("dp", "ctx"), None)
    gains = P(None, ("dp", "ctx"))
    in_specs = (
        (tokens_spec,) * 2 + (P("dp", "ctx"),) * 2 + (matrix,) * 12 + (gains,) * 3 + (P(),) * 3
    )
    out_specs = (tokens_spec,) * 2 + (matrix,) * 12 + (gains,) * 3 + (P(),) * 3
    return jax.shard_map(body, mesh=mesh, in_specs=in_specs, out_specs=out_specs, check_vma=False)
```

time: 4460 us -> 1700 us (0.38)
  waiting for transfers between devices: 3000 us -> 666 us
  matrix products: 730 us -> 357 us
  other arithmetic: 466 us -> 128 us
  Pallas kernels: 0 us -> 126 us
  local copies, waits for them, and re-layouts: 140 us -> 214 us
    unnamed x15 -> x11, waiting for transfers between devices: 1400 us -> 0.18 us
    reduce_scatter x5, waiting for transfers between devices: 1140 us -> 121 us  [the longest x1 121 us: body(): lax.psum_scatter(attention_sum, everyone, scatter_dimension=0, tiled=True)]
    dot_general x124 -> x26, matrix products: 730 us -> 357 us  [dot(): lax.dot_general(left, right, (dims, ((), ())), preferred_element_type=F32)]
    ppermute x0 -> x35, waiting for transfers between devices: none -> 310 us  [the longest x30 196 us: partners(): return lax.ppermute(values, axis, [(i, i ^ shift) for i in range(count)])]
    sub x16 -> x0, other arithmetic: 281 us -> none  [attend_back(): d_probs - inner]
    all_gather x6, waiting for transfers between devices: 468 us -> 235 us  [the longest x1 133 us: body(): lax.all_gather(gate_up_mine.reshape(n_dp * own, 2 * part), 'ctx', axis=0,...]
    pallas_call x0 -> x4, Pallas kernels: none -> 126 us  [the longest x2 85.8 us: attend_back(): pl.pallas_call(functools.partial(attend_back_kernel, turned), grid_spec=p...]
    psum x1, blocking collectives: 40.5 us -> 132 us  [body(): head_grad = lax.psum(sum(head_terms), everyone)]
  transfers between devices with their start and end apart: 13 -> 46, of which waited for: 11 -> 21; matrix products, arithmetic and copies ran while one was open for 11% -> 38% of each run, Pallas kernels for 0% -> 3%
where the time goes in v1:
time: 1700 us; the launch traced here: 1690 us
  waiting for transfers between devices  666 us (39%)
  matrix products  357 us (21%)
  local copies, waits for them, and re-layouts  214 us (13%)
  blocking collectives  132 us (8%)
  other arithmetic  128 us (8%)
  Pallas kernels  126 us (7%)
  starting transfers between devices  41.3 us (2%)
  between operations  22.6 us (1%)
    dot_general x26, matrix products, dot(): lax.dot_general(left, right, (dims, ((), ())), preferred_element_type=F32)  357 us
    ppermute x30, waiting for transfers between devices, partners(): return lax.ppermute(values, axis, [(i, i ^ shift) for i in range(count)])  196 us
    all_gather x1, waiting for transfers between devices, body(): lax.all_gather(gate_up_mine.reshape(n_dp * own, 2 * part), 'ctx', axis=0,...  133 us
    psum x1, blocking collectives, body(): head_grad = lax.psum(sum(head_terms), everyone)  132 us
    reduce_scatter x1, waiting for transfers between devices, body(): lax.psum_scatter(attention_sum, everyone, scatter_dimension=0, tiled=True)  121 us
    ppermute x5, waiting for transfers between devices, mirror(): lax.ppermute(values, 'ctx', [(i, count - 1 - i) for i in range(count)])  114 us
    all_gather x1, waiting for transfers between devices, body(): lax.all_gather((qkv_low * gain_one).astype(LOW), everyone, axis=0, tiled=...  89 us
    pallas_call x2, Pallas kernels, attend_back(): pl.pallas_call(functools.partial(attend_back_kernel, turned), grid_spec=p...  85.8 us
  transfers between devices with their start and end apart: 46, of which 21 were waited for; matrix products, arithmetic and copies ran while one was open for 38% of the time, Pallas kernels for 3%

profile of v1, /device:TPU:0, one launch (start us, length us, event | category | flops | bytes accessed | tf_op | source)
XLA Modules:
  0.0 1687.4 jit_solution(15275296835801519175)
XLA Ops:
  20.6 27.5 %collective-permute-done.10 = s32[2,256]{1,0:T(2,128)S(1)} collective-permute-done((s32[2,256]{1,0:T(2,128)S(1)}, s32[2,256]{1,0:T(2,128)S(1)}, u32[]{:S(2)}, u32[]{:S(2)}) %collective-permute-start.10) | collective-permute-done | bytes 2080 | tf_op jit(solution)/shard_map/ppermute | solution.py:251
  49.9 89.0 %all-gather.9.cloned.1.call-done = bf16[2048,3072]{1,0:T(8,128)(2,1)} async-done(((bf16[64,3072]{1,0:T(8,128)(2,1)}), bf16[2048,3072]{1,0:T(8,128)(2,1)}) %all-gather.9.cloned.1.call-update) | async-done | bytes 12582928 | tf_op jit(solution)/shard_map/all_gather | solution.py:289
  233.9 44.1 %collective-permute-done.24 = bf16[256,2048]{1,0:T(8,128)(2,1)S(1)} collective-permute-done((bf16[256,2048]{1,0:T(8,128)(2,1)S(1)}, bf16[256,2048]{1,0:T(8,128)(2,1)S(1)}, u32[]{:S(2)}, u32[]{:S(2)}) %collective-permute-start.24) | collective-permute-done | bytes 1048608 | tf_op jit(solution)/shard_map/ppermute | solution.py:251
  289.0 15.0 collective-permute-done.25
  304.3 26.9 %collective-permute-done.26 = bf16[256,2048]{1,0:T(8,128)(2,1)S(1)} collective-permute-done((bf16[256,2048]{1,0:T(8,128)(2,1)S(1)}, bf16[256,2048]{1,0:T(8,128)(2,1)S(1)}, u32[]{:S(2)}, u32[]{:S(2)}) %collective-permute-start.26) | collective-permute-done | bytes 1048608 | tf_op jit(solution)/shard_map/ppermute | solution.py:222
  333.4 23.9 %collective-permute-done.18 = bf16[256,2048]{1,0:T(8,128)(2,1)} collective-permute-done((bf16[256,2048]{1,0:T(8,128)(2,1)}, bf16[256,2048]{1,0:T(8,128)(2,1)}, u32[]{:S(2)}, u32[]{:S(2)}) %collective-permute-start.18) | collective-permute-done | bytes 1048608 | tf_op jit(solution)/shard_map/ppermute | solution.py:222
  357.3 14.5 fusion.54
  404.1 33.8 %attend.3 = (bf16[256,2048]{1,0:T(8,128)(2,1)S(1)}, f32[8,1,1024]{2,1,0:T(1,128)S(1)}) custom-call(s32[3]{0:T(128)S(1)} %pad_add_fusion.2.meta_ref, s32[1,1024]{1,0:T(1,128)S(1)} %bitcast.192, s32[1,1024]{1,0:T(1,128)S(1)} %bitcast.190, bf16[8,1024,128]{2,1,0:T(8,128)(2,1)S(1)} %bitcast.182, bf16[8,8,256,128]{3,2,1,0:T(8,128)(2,1)S(1)} %bitcast.197), custom_call_target="tpu_custom_call" | custom-call | flops 8589934592 | bytes 16777216 | tf_op jit(solution)/shard_map/attend/pallas_call | solution.py:174
  486.3 132.8 %all-gather.13.cloned.1.call-done = bf16[2048,4096]{1,0:T(8,128)(2,1)} async-done(((bf16[256,4096]{1,0:T(8,128)(2,1)}), bf16[2048,4096]{1,0:T(8,128)(2,1)}) %all-gather.13.cloned.1.call-update) | async-done | bytes 16777232 | tf_op jit(solution)/shard_map/all_gather | solution.py:294
  619.1 14.7 fusion.6
  633.8 13.7 fusion.2
  647.6 21.7 %multiply_convert_fusion.1 = (bf16[1024,2048]{1,0:T(8,128)(2,1)}, bf16[1024,2048]{1,0:T(8,128)(2,1)}, bf16[1024,2048]{1,0:T(8,128)(2,1)}) fusion(f32[1024,2048]{1,0:T(8,128)} %fusion.6, f32[1024,2048]{1,0:T(8,128)} %fusion.2, bf16[1024,2048]{1,0:T(8,128)(2,1)} %copy-done.88, bf16[2048,2048]{1,0:T(8,128)(2,1)} %all-gather.15.cloned.1.call-done), kind=kOutput, calls=%fused_computation.8 | convolution fusion | flops 8621391872 | bytes 41943040 | tf_op jit(solution)/shard_map/dot_general | solution.py:59
  669.3 23.2 %fusion.17 = bf16[1024,2048]{1,0:T(8,128)(2,1)S(1)} fusion(bf16[2048,4096]{1,0:T(8,128)(2,1)} %all-gather.13.cloned.1.call-done, bf16[1024,2048]{1,0:T(8,128)(2,1)} %get-tuple-element.70, bf16[1024,2048]{1,0:T(8,128)(2,1)} %get-tuple-element.69), kind=kOutput, calls=%fused_computation.40 | convolution fusion | flops 17198743552 | bytes 29360128 | tf_op jit(solution)/shard_map/dot_general | solution.py:59
  715.0 14.7 fusion.4
  729.8 21.7 %multiply_convert_fusion.3 = (bf16[1024,2048]{1,0:T(8,128)(2,1)}, bf16[1024,2048]{1,0:T(8,128)(2,1)}, bf16[1024,2048]{1,0:T(8,128)(2,1)}) fusion(f32[1024,2048]{1,0:T(8,128)} %fusion.54, f32[1024,2048]{1,0:T(8,128)} %fusion.4, bf16[2048,4096]{1,0:T(8,128)(2,1)} %all-gather.13.cloned.1.call-done, bf16[256,2048]{0,1:T(8,128)(2,1)} %collective-permute-done.2, ...), kind=kOutput, calls=%fused_computation.10 | convolution fusion | flops 8638169088 | bytes 41943040 | tf_op jit(solution)/shard_map/dot_general | solution.py:59
  768.7 19.5 %collective-permute-done.15 = bf16[256,2048]{1,0:T(8,128)(2,1)} collective-permute-done((bf16[256,2048]{1,0:T(8,128)(2,1)}, bf16[256,2048]{1,0:T(8,128)(2,1)}, u32[]{:S(2)}, u32[]{:S(2)}) %collective-permute-start.15) | collective-permute-done | bytes 1048608 | tf_op jit(solution)/shard_map/ppermute | solution.py:222
  811.8 73.5 %attend_back.3 = (f32[256,2048]{1,0:T(8,128)S(1)}, bf16[8,8,256,128]{3,2,1,0:T(8,128)(2,1)S(1)}) custom-call(s32[3]{0:T(128)S(1)} %pad_add_fusion.2.meta_ref, s32[1,1024]{1,0:T(1,128)S(1)} %bitcast.193, s32[1,1024]{1,0:T(1,128)S(1)} %bitcast.191, bf16[8,1024,128]{2,1,0:T(8,128)(2,1)S(1)} %bitcast.183, bf16[8,8,256,128]{3,2,1,0:T(8,128)(2,1)} %bitcast.196, ...), custom_call_target="tpu_custom_call" | custom-call | flops 21474836480 | bytes 33554432 | tf_op jit(solution)/shard_map/attend_back/pallas_call | solution.py:199
  888.8 23.6 %fusion.16 = bf16[1024,2048]{1,0:T(8,128)(2,1)S(1)} fusion(bf16[2048,4096]{1,0:T(8,128)(2,1)} %all-gather.13.cloned.1.call-done, bf16[1024,2048]{1,0:T(8,128)(2,1)} %get-tuple-element.67, bf16[1024,2048]{1,0:T(8,128)(2,1)} %get-tuple-element.66), kind=kOutput, calls=%fused_computation.39 | convolution fusion | flops 17198743552 | bytes 29360128 | tf_op jit(solution)/shard_map/dot_general | solution.py:59
  939.8 22.5 %collective-permute-done.22 = bf16[256,2048]{1,0:T(8,128)(2,1)S(1)} collective-permute-done((bf16[256,2048]{1,0:T(8,128)(2,1)S(1)}, bf16[256,2048]{1,0:T(8,128)(2,1)S(1)}, u32[]{:S(2)}, u32[]{:S(2)}) %collective-permute-start.22) | collective-permute-done | bytes 1048608 | tf_op jit(solution)/shard_map/ppermute | solution.py:222
  1036.5 26.2 %fusion.10 = f32[2048,4096]{1,0:T(8,128)} fusion(bf16[1024,2048]{1,0:T(8,128)(2,1)} %get-tuple-element.70, bf16[1024,2048]{1,0:T(8,128)(2,1)} %get-tuple-element.69, bf16[256,2048]{0,1:T(8,128)(2,1)} %collective-permute-done.13, bf16[256,2048]{0,1:T(8,128)(2,1)} %collective-permute-done.12, bf16[256,2048]{0,1:T(8,128)(2,1)} %collective-permute-done.11, ...), kind=kOutput, calls=%fused_computation.26 | convolution fusion | flops 17213423616 | bytes 46137344 | tf_op jit(solution)/shard_map/dot_general | solution.py:59
  1062.7 27.4 %add_convert_fusion = bf16[2048,4096]{1,0:T(8,128)(2,1)} fusion(f32[2048,4096]{1,0:T(8,128)} %fusion.10, bf16[1024,2048]{1,0:T(8,128)(2,1)} %get-tuple-element.67, bf16[1024,2048]{1,0:T(8,128)(2,1)} %get-tuple-element.66, bf16[256,2048]{0,1:T(8,128)(2,1)} %collective-permute-done.2, bf16[256,2048]{0,1:T(8,128)(2,1)} %collective-permute-done.1, ...), kind=kOutput, calls=%fused_computation | convolution fusion | flops 17230200832 | bytes 62914560 | tf_op jit(solution)/shard_map/dot_general | solution.py:59
  1090.2 15.8 fusion.53
  1106.0 14.7 add_convert_fusion.2
  1123.3 13.8 copy.453
  1236.2 15.4 add_convert_fusion.1
  1251.6 17.6 %pad_maximum_fusion = bf16[2048,5120]{1,0:T(8,128)(2,1)} fusion(bf16[2048,2048]{1,0:T(8,128)(2,1)} %add_convert_fusion.3, bf16[2048,3072]{1,0:T(8,128)(2,1)} %add_convert_fusion.1), kind=kLoop, calls=%fused_computation.2 | loop fusion | flops 41943040 | bytes 41943040 | tf_op jit(solution)/shard_map/concatenate | solution.py:429
  1269.5 42.8 %collective-permute-done.17 = bf16[256,2048]{1,0:T(8,128)(2,1)} collective-permute-done((bf16[256,2048]{1,0:T(8,128)(2,1)}, bf16[256,2048]{1,0:T(8,128)(2,1)}, u32[]{:S(2)}, u32[]{:S(2)}) %collective-permute-start.17) | collective-permute-done | bytes 1048608 | tf_op jit(solution)/shard_map/ppermute | solution.py:251
  1325.4 131.6 %psum.7 = f32[2,64]{1,0:T(2,128)S(1)} all-reduce(f32[2,64]{1,0:T(2,128)S(1)} %maximum_add_fusion), channel_id=1, replica_groups=mesh['dp'=4,'ctx'=8] {'dp','ctx'}, use_global_device_ids=true, to_apply=%region_37.38 | all-reduce | flops 128 | bytes 1024 | tf_op jit(solution)/shard_map/psum | solution.py:427
  1483.7 14.6 collective-permute-done.32
  1498.3 20.8 %collective-permute-done.33 = bf16[1,64,4096]{2,1,0:T(8,128)(2,1)S(1)} collective-permute-done((bf16[1,64,4096]{2,1,0:T(8,128)(2,1)}, bf16[1,64,4096]{2,1,0:T(8,128)(2,1)S(1)}, u32[]{:S(2)}, u32[]{:S(2)}) %collective-permute-start.33) | collective-permute-done | bytes 524320 | tf_op jit(solution)/shard_map/ppermute | solution.py:222
  1540.8 13.7 multiply_subtract_fusion
  1554.6 120.7 %reduce-scatter.10.cloned.1.call-done = bf16[64,5120]{1,0:T(8,128)(2,1)} async-done(((bf16[2048,5120]{1,0:T(8,128)(2,1)}), bf16[64,5120]{1,0:T(8,128)(2,1)}) %reduce-scatter.10.cloned.1.call-update) | async-done | bytes 655376 | tf_op jit(solution)/shard_map/reduce_scatter | solution.py:436
  (573 shorter events, 533.1 us)
Async XLA Ops:
  7.2 131.6 %all-gather.9.cloned.1.call-start = ((), (), s32[]{:S(2)}) async-start(), calls=%async_computation.5 | async-start | bytes 12976128 | tf_op jit(solution)/shard_map/all_gather | solution.py:289
  11.2 346.0 %all-gather.15.cloned.1.call-start = ((), (), s32[]{:S(2)}) async-start(), calls=%async_computation.8 | async-start | bytes 9437184 | tf_op jit(solution)/shard_map/all_gather | solution.py:297
  14.0 386.2 %all-gather.19.cloned.1.call-start = ((), (), s32[]{:S(2)}) async-start(), calls=%async_computation.15 | async-start | bytes 4718592 | tf_op jit(solution)/shard_map/all_gather | solution.py:323
  178.9 259.0 %all-gather.11.cloned.1.call-start = ((), (), s32[]{:S(2)}) async-start(), calls=%async_computation.6 | async-start | bytes 8650752 | tf_op jit(solution)/shard_map/all_gather | solution.py:298
  180.8 285.8 %all-gather.17.cloned.1.call-start = ((), (), s32[]{:S(2)}) async-start(), calls=%async_computation.14 | async-start | bytes 4718592 | tf_op jit(solution)/shard_map/all_gather | solution.py:323
  184.6 434.5 %all-gather.13.cloned.1.call-start = ((), (), s32[]{:S(2)}) async-start(), calls=%async_computation.7 | async-start | bytes 18874368 | tf_op jit(solution)/shard_map/all_gather | solution.py:294
  229.3 966.6 %reduce-scatter.8.cloned.1.call-start = ((), (), s32[]{:S(2)}) async-start(), calls=%async_computation.10 | async-start | bytes 4718592 | tf_op jit(solution)/shard_map/reduce_scatter | solution.py:377
  231.0 47.0 %collective-permute-start.24 = (bf16[256,2048]{1,0:T(8,128)(2,1)S(1)}, bf16[256,2048]{1,0:T(8,128)(2,1)S(1)}, u32[]{:S(2)}, u32[]{:S(2)}) collective-permute-start(bf16[256,2048]{1,0:T(8,128)(2,1)S(1)} %get-tuple-element.111), channel_id=1, source_target_pairs={{0,7},{1,6},{2,5},{3,4},{4,3},{5,2},{6,1},{7,0},{8,15},{9,14},{10,... | collective-permute-start | bytes 3145736 | tf_op jit(solution)/shard_map/ppermute | solution.py:251
  231.4 100.0 %collective-permute-start.20 = (bf16[256,2048]{1,0:T(8,128)(2,1)}, bf16[256,2048]{1,0:T(8,128)(2,1)}, u32[]{:S(2)}, u32[]{:S(2)}) collective-permute-start(bf16[256,2048]{1,0:T(8,128)(2,1)} %get-tuple-element.110), channel_id=1, source_target_pairs={{0,24},{8,16},{16,8},{24,0},{1,25},{9,17},{17,9},{25,1},{2,26},{10... | collective-permute-start | bytes 3145736 | tf_op jit(solution)/shard_map/ppermute | solution.py:222
  232.9 100.5 %collective-permute-start.19 = (bf16[256,2048]{1,0:T(8,128)(2,1)}, bf16[256,2048]{1,0:T(8,128)(2,1)}, u32[]{:S(2)}, u32[]{:S(2)}) collective-permute-start(bf16[256,2048]{1,0:T(8,128)(2,1)} %get-tuple-element.110), channel_id=1, source_target_pairs={{0,16},{8,24},{16,0},{24,8},{1,17},{9,25},{17,1},{25,9},{2,18},{10... | collective-permute-start | bytes 3145736 | tf_op jit(solution)/shard_map/ppermute | solution.py:222
  281.5 49.7 %collective-permute-start.26 = (bf16[256,2048]{1,0:T(8,128)(2,1)S(1)}, bf16[256,2048]{1,0:T(8,128)(2,1)S(1)}, u32[]{:S(2)}, u32[]{:S(2)}) collective-permute-start(bf16[256,2048]{1,0:T(8,128)(2,1)S(1)} %collective-permute-done.24), channel_id=1, source_target_pairs={{0,16},{8,24},{16,0},{24,8},{1,17},{9,25},{17,1},{25,9},{2,18},{10... | collective-permute-start | bytes 3145736 | tf_op jit(solution)/shard_map/ppermute | solution.py:222
  304.1 53.2 %collective-permute-start.18 = (bf16[256,2048]{1,0:T(8,128)(2,1)}, bf16[256,2048]{1,0:T(8,128)(2,1)}, u32[]{:S(2)}, u32[]{:S(2)}) collective-permute-start(bf16[256,2048]{1,0:T(8,128)(2,1)} %get-tuple-element.110), channel_id=1, source_target_pairs={{0,8},{8,0},{16,24},{24,16},{1,9},{9,1},{17,25},{25,17},{2,10},{10... | collective-permute-start | bytes 3145736 | tf_op jit(solution)/shard_map/ppermute | solution.py:222
  451.5 167.6 %collective-permute-start.12 = (bf16[256,2048]{0,1:T(8,128)(2,1)}, bf16[256,2048]{0,1:T(8,128)(2,1)}, u32[]{:S(2)}, u32[]{:S(2)}) collective-permute-start(bf16[256,2048]{0,1:T(8,128)(2,1)} %bitcast.43), channel_id=1, source_target_pairs={{0,16},{8,24},{16,0},{24,8},{1,17},{9,25},{17,1},{25,9},{2,18},{10... | collective-permute-start | bytes 3145736 | tf_op jit(solution)/shard_map/ppermute | solution.py:222
  451.5 167.6 %collective-permute-start.11 = (bf16[256,2048]{0,1:T(8,128)(2,1)}, bf16[256,2048]{0,1:T(8,128)(2,1)}, u32[]{:S(2)}, u32[]{:S(2)}) collective-permute-start(bf16[256,2048]{0,1:T(8,128)(2,1)} %bitcast.43), channel_id=1, source_target_pairs={{0,8},{8,0},{16,24},{24,16},{1,9},{9,1},{17,25},{25,17},{2,10},{10... | collective-permute-start | bytes 3145736 | tf_op jit(solution)/shard_map/ppermute | solution.py:222
  482.8 228.7 %collective-permute-start.2 = (bf16[256,2048]{0,1:T(8,128)(2,1)}, bf16[256,2048]{0,1:T(8,128)(2,1)}, u32[]{:S(2)}, u32[]{:S(2)}) collective-permute-start(bf16[256,2048]{0,1:T(8,128)(2,1)} %bitcast.20), channel_id=1, source_target_pairs={{0,24},{8,16},{16,8},{24,0},{1,25},{9,17},{17,9},{25,1},{2,26},{10... | collective-permute-start | bytes 3145736 | tf_op jit(solution)/shard_map/ppermute | solution.py:222
  485.2 227.8 %collective-permute-start.1 = (bf16[256,2048]{0,1:T(8,128)(2,1)}, bf16[256,2048]{0,1:T(8,128)(2,1)}, u32[]{:S(2)}, u32[]{:S(2)}) collective-permute-start(bf16[256,2048]{0,1:T(8,128)(2,1)} %bitcast.20), channel_id=1, source_target_pairs={{0,16},{8,24},{16,0},{24,8},{1,17},{9,25},{17,1},{25,9},{2,18},{10... | collective-permute-start | bytes 3145736 | tf_op jit(solution)/shard_map/ppermute | solution.py:222
  485.8 228.7 %collective-permute-start = (bf16[256,2048]{0,1:T(8,128)(2,1)}, bf16[256,2048]{0,1:T(8,128)(2,1)}, u32[]{:S(2)}, u32[]{:S(2)}) collective-permute-start(bf16[256,2048]{0,1:T(8,128)(2,1)} %bitcast.20), channel_id=1, source_target_pairs={{0,8},{8,0},{16,24},{24,16},{1,9},{9,1},{17,25},{25,17},{2,10},{10... | collective-permute-start | bytes 3145736 | tf_op jit(solution)/shard_map/ppermute | solution.py:222
  694.2 57.2 %collective-permute-start.30 = (bf16[256,2048]{1,0:T(8,128)(2,1)}, bf16[256,2048]{1,0:T(8,128)(2,1)S(1)}, u32[]{:S(2)}, u32[]{:S(2)}) collective-permute-start(bf16[256,2048]{1,0:T(8,128)(2,1)} %get-tuple-element.85), channel_id=1, source_target_pairs={{0,24},{8,16},{16,8},{24,0},{1,25},{9,17},{17,9},{25,1},{2,26},{10... | collective-permute-start | bytes 3145736 | tf_op jit(solution)/shard_map/ppermute | solution.py:222
  696.6 56.4 %collective-permute-start.29 = (bf16[256,2048]{1,0:T(8,128)(2,1)}, bf16[256,2048]{1,0:T(8,128)(2,1)}, u32[]{:S(2)}, u32[]{:S(2)}) collective-permute-start(bf16[256,2048]{1,0:T(8,128)(2,1)} %get-tuple-element.86), channel_id=1, source_target_pairs={{0,16},{8,24},{16,0},{24,8},{1,17},{9,25},{17,1},{25,9},{2,18},{10... | collective-permute-start | bytes 3145736 | tf_op jit(solution)/shard_map/ppermute | solution.py:222
  713.0 55.7 %collective-permute-start.16 = (bf16[256,2048]{1,0:T(8,128)(2,1)}, bf16[256,2048]{1,0:T(8,128)(2,1)}, u32[]{:S(2)}, u32[]{:S(2)}) collective-permute-start(bf16[256,2048]{1,0:T(8,128)(2,1)} %get-tuple-element.91), channel_id=1, source_target_pairs={{0,24},{8,16},{16,8},{24,0},{1,25},{9,17},{17,9},{25,1},{2,26},{10... | collective-permute-start | bytes 3145736 | tf_op jit(solution)/shard_map/ppermute | solution.py:222
  714.5 73.7 %collective-permute-start.15 = (bf16[256,2048]{1,0:T(8,128)(2,1)}, bf16[256,2048]{1,0:T(8,128)(2,1)}, u32[]{:S(2)}, u32[]{:S(2)}) collective-permute-start(bf16[256,2048]{1,0:T(8,128)(2,1)} %get-tuple-element.92), channel_id=1, source_target_pairs={{0,16},{8,24},{16,0},{24,8},{1,17},{9,25},{17,1},{25,9},{2,18},{10... | collective-permute-start | bytes 3145736 | tf_op jit(solution)/shard_map/ppermute | solution.py:222
  888.8 310.6 %reduce-scatter.6.cloned.1.call-start = ((), (), s32[]{:S(2)}) async-start(), calls=%async_computation.9 | async-start | bytes 4718592 | tf_op jit(solution)/shard_map/reduce_scatter | solution.py:377
  914.4 47.9 %collective-permute-start.22 = (bf16[256,2048]{1,0:T(8,128)(2,1)S(1)}, bf16[256,2048]{1,0:T(8,128)(2,1)S(1)}, u32[]{:S(2)}, u32[]{:S(2)}) collective-permute-start(bf16[256,2048]{1,0:T(8,128)(2,1)S(1)} %get-tuple-element.83), channel_id=1, source_target_pairs={{0,16},{8,24},{16,0},{24,8},{1,17},{9,25},{17,1},{25,9},{2,18},{10... | collective-permute-start | bytes 3145736 | tf_op jit(solution)/shard_map/ppermute | solution.py:222
  914.4 47.9 %collective-permute-start.21 = (bf16[256,2048]{1,0:T(8,128)(2,1)S(1)}, bf16[256,2048]{1,0:T(8,128)(2,1)S(1)}, u32[]{:S(2)}, u32[]{:S(2)}) collective-permute-start(bf16[256,2048]{1,0:T(8,128)(2,1)S(1)} %get-tuple-element.81), channel_id=1, source_target_pairs={{0,8},{8,0},{16,24},{24,16},{1,9},{9,1},{17,25},{25,17},{2,10},{10... | collective-permute-start | bytes 3145736 | tf_op jit(solution)/shard_map/ppermute | solution.py:222
  931.2 53.8 %collective-permute-start.8 = (bf16[256,2048]{1,0:T(8,128)(2,1)}, bf16[256,2048]{1,0:T(8,128)(2,1)}, u32[]{:S(2)}, u32[]{:S(2)}) collective-permute-start(bf16[256,2048]{1,0:T(8,128)(2,1)} %get-tuple-element.88), channel_id=1, source_target_pairs={{0,24},{8,16},{16,8},{24,0},{1,25},{9,17},{17,9},{25,1},{2,26},{10... | collective-permute-start | bytes 3145736 | tf_op jit(solution)/shard_map/ppermute | solution.py:222
  932.8 64.3 %collective-permute-start.7 = (bf16[256,2048]{1,0:T(8,128)(2,1)}, bf16[256,2048]{1,0:T(8,128)(2,1)}, u32[]{:S(2)}, u32[]{:S(2)}) collective-permute-start(bf16[256,2048]{1,0:T(8,128)(2,1)} %get-tuple-element.89), channel_id=1, source_target_pairs={{0,16},{8,24},{16,0},{24,8},{1,17},{9,25},{17,1},{25,9},{2,18},{10... | collective-permute-start | bytes 3145736 | tf_op jit(solution)/shard_map/ppermute | solution.py:222
  939.8 57.2 %collective-permute-start.6 = (bf16[256,2048]{1,0:T(8,128)(2,1)S(1)}, bf16[256,2048]{1,0:T(8,128)(2,1)}, u32[]{:S(2)}, u32[]{:S(2)}) collective-permute-start(bf16[256,2048]{1,0:T(8,128)(2,1)S(1)} %get-tuple-element.87), channel_id=1, source_target_pairs={{0,8},{8,0},{16,24},{24,16},{1,9},{9,1},{17,25},{25,17},{2,10},{10... | collective-permute-start | bytes 3145736 | tf_op jit(solution)/shard_map/ppermute | solution.py:222
  1036.5 432.3 %reduce-scatter.12.cloned.1.call-start = ((), (), s32[]{:S(2)}) async-start(), calls=%async_computation.12 | async-start | bytes 18874368 | tf_op jit(solution)/shard_map/reduce_scatter | solution.py:410
  1090.1 386.4 %reduce-scatter.14.cloned.1.call-start = ((), (), s32[]{:S(2)}) async-start(), calls=%async_computation.13 | async-start | bytes 9437184 | tf_op jit(solution)/shard_map/reduce_scatter | solution.py:416
  1120.7 554.6 %reduce-scatter.10.cloned.1.call-start = ((), (), s32[]{:S(2)}) async-start(), calls=%async_computation.11 | async-start | bytes 21626880 | tf_op jit(solution)/shard_map/reduce_scatter | solution.py:436
  1323.6 143.7 %collective-permute-start.31 = (bf16[256,2048]{1,0:T(8,128)(2,1)}, bf16[256,2048]{1,0:T(8,128)(2,1)S(1)}, u32[]{:S(2)}, u32[]{:S(2)}) collective-permute-start(bf16[256,2048]{1,0:T(8,128)(2,1)} %fusion.31), channel_id=1, source_target_pairs={{0,7},{1,6},{2,5},{3,4},{4,3},{5,2},{6,1},{7,0},{8,15},{9,14},{10,... | collective-permute-start | bytes 3145736 | tf_op jit(solution)/shard_map/ppermute | solution.py:251
  1474.1 45.1 %collective-permute-start.33 = (bf16[1,64,4096]{2,1,0:T(8,128)(2,1)}, bf16[1,64,4096]{2,1,0:T(8,128)(2,1)S(1)}, u32[]{:S(2)}, u32[]{:S(2)}) collective-permute-start(bf16[1,64,4096]{2,1,0:T(8,128)(2,1)} %get-tuple-element.103), channel_id=1, source_target_pairs={{0,16},{8,24},{16,0},{24,8},{1,17},{9,25},{17,1},{25,9},{2,18},{10... | collective-permute-start | bytes 1572872 | tf_op jit(solution)/shard_map/ppermute | solution.py:222
  (143 other events, 3395.9 us)
Sparse Core Ops, SparseCore 0:
  11.6 127.1 all-gather.8
  141.0 80.2 all-gather.14
  223.6 84.5 all-gather.18
  311.6 106.2 all-gather.10
  420.0 46.6 all-gather.16
  468.7 150.3 all-gather.12
  888.9 47.4 reduce-scatter.7
  1036.6 55.7 reduce-scatter.5
  1094.7 169.4 reduce-scatter.11
  1266.3 155.3 reduce-scatter.13
  1424.1 251.2 reduce-scatter.9

commit v2 on v1

v2 whole, which is shorter than its diff:
```python
import functools
import math

import jax
import jax.numpy as jnp
from jax import lax
from jax.experimental import pallas as pl
from jax.experimental.pallas import tpu as pltpu
from jax.sharding import PartitionSpec as P

H = 32
KV = 8
HD = 64
G = H // KV
STEP = 5

EPS = 1e-05
ROPE_BASE = 1000000.0
BETA_ONE = 0.9
BETA_TWO = 0.95
ADAM_EPS = 1e-08
DECAY = 0.1
RATE_QKV = 0.05
RATE_OUT = 0.3
RATE_GATE_UP = 0.05
RATE_DOWN = 0.03
RATE_GAIN = 0.5

LOW = jnp.bfloat16
F32 = jnp.float32


def rms_scale(values):
    return lax.rsqrt(jnp.mean(values * values, axis=-1, keepdims=True) + EPS)


def norm_back(scaled, values, inv_rms):
    inner = jnp.mean(scaled * values, axis=-1, keepdims=True)
    return inv_rms * (scaled - values * inv_rms * inv_rms * inner)


def rotary(values, cosine, sine):
    first, second = values[..., : HD // 2], values[..., HD // 2 :]
    return jnp.concatenate([first * cosine - second * sine, second * cosine + first * sine], axis=-1)


def rotary_back(grad, cosine, sine):
    first, second = grad[..., : HD // 2], grad[..., HD // 2 :]
    return jnp.concatenate([first * cosine + second * sine, second * cosine - first * sine], axis=-1)


def rotary_tables(place_ids):
    freqs = ROPE_BASE ** (-(jnp.arange(HD // 2).astype(F32) * 2.0 / HD))
    angles = place_ids.astype(F32)[..., None] * freqs
    return (jnp.cos(angles), jnp.sin(angles))


def dot(left, right, dims):
    return lax.dot_general(left, right, (dims, ((), ())), preferred_element_type=F32)


NN = ((1,), (0,))
NT = ((1,), (1,))
TN = ((0,), (0,))


def adam(master, moment_one, moment_two, grad, step_rate, decay_rate):
    first_new = BETA_ONE * moment_one + (1.0 - BETA_ONE) * grad
    second_new = BETA_TWO * moment_two + (1.0 - BETA_TWO) * grad * grad
    first_hat = first_new / (1.0 - BETA_ONE**STEP)
    second_hat = second_new / (1.0 - BETA_TWO**STEP)
    master_new = master - step_rate * (
        first_hat / (jnp.sqrt(second_hat) + ADAM_EPS) + decay_rate * master
    )
    return (master_new, first_new, second_new)


def chunk_mask(chunk, length, start, query_index):
    key_index = chunk * length + lax.broadcasted_iota(jnp.int32, (length, start.shape[1]), 0)
    return (key_index >= start) & (key_index <= query_index)


def for_chunks(meta_ref, step):
    block = pl.program_id(0)
    place, low, full = meta_ref[block, 0], meta_ref[block, 1], meta_ref[block, 2]

    @pl.loop(low, full)
    def _(chunk):
        step(chunk, True)

    @pl.loop(full, place)
    def _(chunk):
        step(chunk, False)

    step(place, True)


def attend_kernel(meta_ref, start_ref, index_ref, query_ref, kv_ref, out_ref, log_ref, acc_ref):
    length = query_ref.shape[2] // G
    start, query_index = start_ref[0], index_ref[0]
    turned = meta_ref[pl.program_id(0), 3]
    lane = lax.broadcasted_iota(jnp.int32, (length, 2 * HD), 1)
    acc_ref[...] = jnp.zeros_like(acc_ref)

    def step(chunk, masked):
        slot = chunk + turned * (kv_ref.shape[0] - 1 - 2 * chunk)
        kv = kv_ref[slot, 0, 0]
        ones_v = jnp.where(lane < HD, jnp.ones_like(kv), kv)
        probs = jnp.exp(dot(kv, query_ref[0, 0], NT))
        if masked:
            probs = jnp.where(chunk_mask(chunk, length, start, query_index), probs, 0.0)
        acc_ref[...] += dot(ones_v, probs.astype(LOW), TN)

    for_chunks(meta_ref, step)
    total = acc_ref[:1, :]
    log_ref[0, 0] = jnp.log(total)
    mixed = acc_ref[HD:, :] / total
    rows = [mixed[:, head * length : (head + 1) * length] for head in range(G)]
    out_ref[0] = jnp.concatenate(rows, axis=0).T.astype(out_ref.dtype)


def attend_back_kernel(
    meta_ref,
    start_ref,
    index_ref,
    query_ref,
    kv_ref,
    grad_ref,
    log_ref,
    inner_ref,
    _,
    dq_ref,
    dkv_ref,
    acc_ref,
):
    length = query_ref.shape[2] // G
    start, query_index = start_ref[0], index_ref[0]
    turned = meta_ref[pl.program_id(0), 3]
    acc_ref[...] = jnp.zeros_like(acc_ref)
    dkv_ref[...] = jnp.zeros_like(dkv_ref)

    def step(chunk, masked):
        slot = chunk + turned * (kv_ref.shape[0] - 1 - 2 * chunk)
        kv = kv_ref[slot, 0, 0]
        total = jnp.zeros((length, 2 * HD), F32)
        for head in range(G):
            part = pl.ds(head * length, length)
            query, grad = query_ref[0, 0, part], grad_ref[0, 0, part]
            probs = jnp.exp(dot(kv, query, NT) - log_ref[0, 0, :, part])
            if masked:
                mask = chunk_mask(chunk, length, start[:, :length], query_index[:, :length])
                probs = jnp.where(mask, probs, 0.0)
            d_probs = dot(kv, grad, NT)
            d_scores = (probs * (d_probs - inner_ref[0, 0, :, part])).astype(LOW)
            total = total + dot(d_scores, query, NN) + dot(probs.astype(LOW), grad, NN)
            acc_ref[:, part] += dot(kv, d_scores, TN)
        dkv_ref[slot, 0, 0] = total.astype(dkv_ref.dtype)

    for_chunks(meta_ref, step)
    rows = [acc_ref[:HD, head * length : (head + 1) * length] for head in range(G)]
    dq_ref[0] = jnp.concatenate(rows, axis=0).T * (1.0 / math.sqrt(HD))


def attention_specs(n_ctx, length):
    query = pl.BlockSpec((1, 1, G * length, 2 * HD), lambda b, h, *_: (b, h, 0, 0))
    kv = pl.BlockSpec((n_ctx, 1, 1, length, 2 * HD), lambda b, h, *_: (0, b, h, 0, 0))
    row = pl.BlockSpec((1, 1, 1, G * length), lambda b, h, *_: (b, h, 0, 0))
    start = pl.BlockSpec((1, 1, G * length), lambda b, h, *_: (b, 0, 0))
    natural = pl.BlockSpec((1, length, G * HD), lambda b, h, *_: (b, 0, h))
    return query, kv, row, start, natural


def attend(meta, start, index, query, kv_all):
    n_ctx, blocks, heads, length, _ = kv_all.shape
    q_spec, kv_spec, row_spec, start_spec, natural = attention_specs(n_ctx, length)
    pairs = blocks * heads * G * length * n_ctx * length
    return pl.pallas_call(
        attend_kernel,
        grid_spec=pltpu.PrefetchScalarGridSpec(
            num_scalar_prefetch=1,
            grid=(blocks, heads),
            in_specs=[start_spec, start_spec, q_spec, kv_spec],
            out_specs=[natural, row_spec],
            scratch_shapes=[pltpu.VMEM((2 * HD, G * length), F32)],
        ),
        out_shape=[
            jax.ShapeDtypeStruct((blocks, length, heads * G * HD), LOW),
            jax.ShapeDtypeStruct((blocks, heads, 1, G * length), F32),
        ],
        compiler_params=pltpu.CompilerParams(vmem_limit_bytes=40 * 2**20),
        cost_estimate=pl.CostEstimate(
            flops=pairs * 32, bytes_accessed=2**20, transcendentals=0
        ),
        name="attend",
    )(meta, start, index, query, kv_all)


def attend_back(meta, start, index, query, kv_all, grad, log_total, inner, other):
    n_ctx, blocks, heads, length, _ = kv_all.shape
    q_spec, kv_spec, row_spec, start_spec, natural = attention_specs(n_ctx, length)
    pairs = blocks * heads * G * length * n_ctx * length
    return pl.pallas_call(
        attend_back_kernel,
        grid_spec=pltpu.PrefetchScalarGridSpec(
            num_scalar_prefetch=1,
            grid=(blocks, heads),
            in_specs=[start_spec, start_spec, q_spec, kv_spec, q_spec, row_spec, row_spec]
            + [pl.BlockSpec(memory_space=pl.ANY)],
            out_specs=[natural, kv_spec],
            scratch_shapes=[pltpu.VMEM((2 * HD, G * length), F32)],
        ),
        out_shape=[
            jax.ShapeDtypeStruct((blocks, length, heads * G * HD), F32),
            jax.ShapeDtypeStruct(kv_all.shape, LOW),
        ],
        compiler_params=pltpu.CompilerParams(vmem_limit_bytes=40 * 2**20),
        cost_estimate=pl.CostEstimate(
            flops=pairs * 64, bytes_accessed=2**20, transcendentals=0
        ),
        name="attend_back",
    )(meta, start, index, query, kv_all, grad, log_total, inner, other)


MESH = pl.DeviceIdType.MESH
DMA = pltpu.SemaphoreType.DMA


def flip(rank, shift):
    result, bit = rank, 1
    while bit <= shift:
        if shift & bit:
            result = result + bit - 2 * bit * ((rank // bit) % 2)
        bit *= 2
    return result


class Place:
    def __init__(self, n_dp, n_ctx):
        self.n_dp, self.n_ctx = n_dp, n_ctx
        self.last = n_ctx // 2 - 1
        self.dp, self.ctx = lax.axis_index("dp"), lax.axis_index("ctx")
        self.column, self.core = self.ctx // 2, self.ctx % 2
        self.sibling = (self.dp, self.ctx + 1 - 2 * self.core)
        self.above = (self.dp, self.ctx + 2)
        self.below = (self.dp, self.ctx - 2)
        self.opposite = (self.dp, n_ctx - 1 - self.ctx)

    def peer(self, shift):
        return (flip(self.dp, shift), self.ctx)

    def meet(self, along_dp, along_ctx, across):
        barrier = pltpu.get_barrier_semaphore()

        def greet(device):
            pl.semaphore_signal(barrier, inc=1, device_id=device, device_id_type=MESH)

        count = 0
        if across:
            greet(self.opposite)
            count = 1
        if along_dp:
            for shift in range(1, self.n_dp):
                greet(self.peer(shift))
            count = count + self.n_dp - 1
        if along_ctx:
            greet(self.sibling)
            count = count + 1
            if self.last > 0:
                pl.when(self.column > 0)(lambda: greet(self.below))
                pl.when(self.column < self.last)(lambda: greet(self.above))
                count = count + (self.column + self.last - 1) // self.last
                count = count + (2 * self.last - 1 - self.column) // self.last
        pl.semaphore_wait(barrier, count)


def remote(source, target, send_sem, recv_sem, device):
    return pltpu.make_async_remote_copy(
        src_ref=source,
        dst_ref=target,
        send_sem=send_sem,
        recv_sem=recv_sem,
        device_id=device,
        device_id_type=MESH,
    )


CHUNKS = 2


class GatherDp:
    along_dp, along_ctx, across = True, False, False

    def __init__(self, values, n_dp, n_ctx):
        self.rows = values.shape[0]
        self.operand_spec = pl.BlockSpec(memory_space=pl.ANY)
        self.out_spec = pl.BlockSpec(memory_space=pl.ANY)
        self.out_shape = jax.ShapeDtypeStruct((n_dp, *values.shape), values.dtype)
        self.scratch = [DMA(()), DMA((n_dp, CHUNKS, 2)), DMA((n_dp, CHUNKS, 2))]

    def phases(self, at, own, out, local, send, recv):
        size = self.rows // CHUNKS
        halves = at.n_dp == 4
        direct = (1, 2) if halves else tuple(range(1, at.n_dp))
        mine = pltpu.make_async_copy(own, out.at[0], local)

        def straight(shift, chunk):
            part = pl.ds(chunk * size, size)
            return remote(
                own.at[part],
                out.at[shift, part],
                send.at[shift, chunk, 0],
                recv.at[shift, chunk, 0],
                at.peer(shift),
            )

        def turned(shift, chunk):
            part = pl.ds(chunk * size + (2 - shift) * (size // 2), size // 2)
            return remote(
                out.at[3 - shift, part],
                out.at[3, part],
                send.at[3, chunk, shift - 1],
                recv.at[3, chunk, shift - 1],
                at.peer(shift),
            )

        def begin():
            for chunk in range(CHUNKS):
                for shift in direct:
                    straight(shift, chunk).start()
            mine.start()

        def middle():
            for chunk in range(CHUNKS):
                for shift in direct:
                    straight(shift, chunk).wait_recv()
                    if halves:
                        turned(3 - shift, chunk).start()

        def end():
            for chunk in range(CHUNKS):
                if halves:
                    for shift in direct:
                        turned(shift, chunk).wait()
                for shift in direct:
                    straight(shift, chunk).wait_send()
            mine.wait()

        return [begin, middle, end]


class SumDp:
    along_dp, along_ctx, across = True, False, False

    def __init__(self, values, n_dp, n_ctx):
        _, self.rows, width = values.shape
        size = self.rows // CHUNKS
        self.operand_spec = pl.BlockSpec(memory_space=pltpu.VMEM)
        self.out_spec = pl.BlockSpec(memory_space=pltpu.VMEM)
        self.out_shape = jax.ShapeDtypeStruct((self.rows, width), F32)
        peers = 2 if n_dp == 4 else n_dp - 1
        self.scratch = [
            pltpu.VMEM((2, CHUNKS, size // 2, width), LOW),
            pltpu.VMEM((2, CHUNKS, size // 2, width), LOW),
            pltpu.VMEM((peers, CHUNKS, 2, size // 2, width), LOW),
            DMA((2, CHUNKS)),
            DMA((2, CHUNKS)),
            DMA((peers, CHUNKS, 2)),
            DMA((peers, CHUNKS, 2)),
        ]

    def phases(self, at, parts, out, arrived, joined, sums, t_send, t_recv, p_send, p_recv):
        size = self.rows // CHUNKS
        half = size // 2
        halves = at.n_dp == 4
        direct = (1, 2) if halves else tuple(range(1, at.n_dp))

        def rows(chunk, which):
            return pl.ds(chunk * size + which * half, half)

        def turning(shift, chunk):
            return remote(
                parts.at[3, rows(chunk, shift - 1)],
                arrived.at[shift - 1, chunk],
                t_send.at[shift - 1, chunk],
                t_recv.at[shift - 1, chunk],
                at.peer(shift),
            )

        def final(shift, chunk, which):
            source = parts.at[shift, rows(chunk, which)]
            if halves and which == 2 - shift:
                source = joined.at[shift - 1, chunk]
            return remote(
                source,
                sums.at[shift - 1, chunk, which],
                p_send.at[shift - 1, chunk, which],
                p_recv.at[shift - 1, chunk, which],
                at.peer(shift),
            )

        def begin():
            for chunk in range(CHUNKS):
                if halves:
                    for shift in direct:
                        turning(shift, chunk).start()
                for shift in direct:
                    for which in (0, 1):
                        if not halves or which != 2 - shift:
                            final(shift, chunk, which).start()

        def middle():
            if halves:
                for chunk in range(CHUNKS):
                    for shift in direct:
                        turning(shift, chunk).wait_recv()
                        to = 3 - shift
                        mine = parts[to, rows(chunk, shift - 1)].astype(F32)
                        came = arrived[shift - 1, chunk].astype(F32)
                        joined[to - 1, chunk] = (mine + came).astype(LOW)
                        final(to, chunk, shift - 1).start()

        def end():
            for chunk in range(CHUNKS):
                for which in (0, 1):
                    total = parts[0, rows(chunk, which)].astype(F32)
                    for shift in direct:
                        final(shift, chunk, which).wait_recv()
                        total = total + sums[shift - 1, chunk, which].astype(F32)
                    out[rows(chunk, which)] = total
            for chunk in range(CHUNKS):
                for shift in direct:
                    if halves:
                        turning(shift, chunk).wait_send()
                    for which in (0, 1):
                        final(shift, chunk, which).wait_send()

        return [begin, middle, end]


class GatherCtx:
    along_dp, along_ctx, across = False, True, False

    def __init__(self, values, n_dp, n_ctx):
        columns = n_ctx // 2
        self.operand_spec = pl.BlockSpec(memory_space=pl.ANY)
        self.out_spec = pl.BlockSpec(memory_space=pl.ANY)
        self.out_shape = jax.ShapeDtypeStruct((n_ctx, *values.shape), values.dtype)
        self.scratch = [DMA(())] + [DMA((columns,))] * 5

    def phases(self, at, own, out, local, up_send, down_send, recv, sib_send, sib_recv):
        mine = pltpu.make_async_copy(own, out.at[at.ctx], local)

        def travel(column, sem, device):
            ref = out.at[2 * column + at.core]
            source = ref
            return remote(source, ref, sem.at[column], recv.at[column], device)

        def to_sibling(column):
            ref = out.at[2 * column + at.core]
            return remote(ref, ref, sib_send.at[column], sib_recv.at[column], at.sibling)

        def from_sibling(column):
            ref = out.at[2 * column + 1 - at.core]
            remote(ref, ref, sib_send.at[column], sib_recv.at[column], at.sibling).wait_recv()

        def pass_on(column):
            pl.when((column <= at.column) & (at.column < at.last))(
                lambda: travel(column, up_send, at.above).start()
            )
            pl.when((column >= at.column) & (at.column > 0))(
                lambda: travel(column, down_send, at.below).start()
            )
            to_sibling(column).start()

        def begin():
            mine.start()
            mine.wait()
            pass_on(at.column)

        def middle():
            @pl.loop(1, 2 * at.last + 1)
            def _(count):
                away = (count + 1) // 2
                column = at.column + away - 2 * away * (count % 2)

                @pl.when((column >= 0) & (column <= at.last))
                def _():
                    travel(column, up_send, at.sibling).wait_recv()
                    pass_on(column)

        def end():
            @pl.loop(0, at.last + 1)
            def _(column):
                from_sibling(column)
                to_sibling(column).wait_send()
                pl.when((column <= at.column) & (at.column < at.last))(
                    lambda: travel(column, up_send, at.above).wait_send()
                )
                pl.when((column >= at.column) & (at.column > 0))(
                    lambda: travel(column, down_send, at.below).wait_send()
                )

        return [begin, middle, end]


class SumCtx:
    along_dp, along_ctx, across = False, True, False

    def __init__(self, values, n_dp, n_ctx):
        columns = n_ctx // 2
        _, rows, width = values.shape
        self.operand_spec = pl.BlockSpec(memory_space=pltpu.VMEM)
        self.out_spec = pl.BlockSpec(memory_space=pltpu.VMEM)
        self.out_shape = jax.ShapeDtypeStruct((rows, width), F32)
        block = pltpu.VMEM((columns, rows, width), LOW)
        self.scratch = [block] * 4 + [DMA((columns,))] * 6

    def phases(
        self,
        at,
        parts,
        out,
        acc,
        from_sib,
        from_below,
        from_above,
        sib_send,
        sib_recv,
        up_send,
        up_recv,
        down_send,
        down_recv,
    ):
        def to_sibling(column):
            return remote(
                parts.at[2 * column + 1 - at.core],
                from_sib.at[column],
                sib_send.at[column],
                sib_recv.at[column],
                at.sibling,
            )

        def to_above(column):
            return remote(
                acc.at[column],
                from_below.at[column],
                up_send.at[column],
                up_recv.at[column],
                at.above,
            )

        def to_below(column):
            return remote(
                acc.at[column],
                from_above.at[column],
                down_send.at[column],
                down_recv.at[column],
                at.below,
            )

        def farthest_first(step):
            @pl.loop(0, at.last + 1)
            def _(count):
                odd = count % 2
                step((1 - odd) * (at.last - count // 2) + odd * (count // 2))

        def begin():
            farthest_first(lambda column: to_sibling(column).start())

        def line(column):
            to_sibling(column).wait_recv()
            mine = parts[2 * column + at.core].astype(F32) + from_sib[column].astype(F32)
            acc[column] = mine.astype(LOW)

            def add(came):
                acc[column] = (acc[column].astype(F32) + came[column].astype(F32)).astype(LOW)

            @pl.when(column > at.column)
            def _():
                @pl.when(at.column > 0)
                def _():
                    to_above(column).wait_recv()
                    add(from_below)

                to_above(column).start()

            @pl.when(column < at.column)
            def _():
                @pl.when(at.column < at.last)
                def _():
                    to_below(column).wait_recv()
                    add(from_above)

                to_below(column).start()

        def middle():
            farthest_first(line)

        def end():
            out[...] = acc[at.column].astype(F32)

            @pl.when(at.column > 0)
            def _():
                to_above(at.column).wait_recv()
                out[...] += from_below[at.column].astype(F32)

            @pl.when(at.column < at.last)
            def _():
                to_below(at.column).wait_recv()
                out[...] += from_above[at.column].astype(F32)

            @pl.loop(0, at.last + 1)
            def _(column):
                to_sibling(column).wait_send()
                pl.when(column > at.column)(lambda: to_above(column).wait_send())
                pl.when(column < at.column)(lambda: to_below(column).wait_send())

        return [begin, middle, end]


class Mirror:
    along_dp, along_ctx, across = False, False, True

    def __init__(self, values, n_dp, n_ctx):
        self.operand_spec = pl.BlockSpec(memory_space=pl.ANY)
        self.out_spec = pl.BlockSpec(memory_space=pl.ANY)
        self.out_shape = jax.ShapeDtypeStruct(values.shape, values.dtype)
        self.scratch = [DMA(()), DMA(())]

    def phases(self, at, own, out, send, recv):
        copy = remote(own, out, send, recv, at.opposite)
        return [copy.start, lambda: None, copy.wait]


class ExchangeDp:
    along_dp, along_ctx, across = True, False, False

    def __init__(self, values, n_dp, n_ctx):
        self.operand_spec = pl.BlockSpec(memory_space=pl.ANY)
        self.out_spec = pl.BlockSpec(memory_space=pl.ANY)
        self.out_shape = jax.ShapeDtypeStruct(values.shape, values.dtype)
        self.scratch = [DMA(()), DMA((n_dp,)), DMA((n_dp,))]

    def phases(self, at, blocks, out, local, send, recv):
        mine = pltpu.make_async_copy(blocks.at[at.dp], out.at[at.dp], local)

        def to_peer(shift):
            return remote(
                blocks.at[flip(at.dp, shift)],
                out.at[at.dp],
                send.at[shift],
                recv.at[shift],
                at.peer(shift),
            )

        def from_peer(shift):
            ref = out.at[flip(at.dp, shift)]
            return remote(ref, ref, send.at[shift], recv.at[shift], at.peer(shift))

        def begin():
            for shift in range(1, at.n_dp):
                to_peer(shift).start()
            mine.start()

        def end():
            for shift in range(1, at.n_dp):
                from_peer(shift).wait_recv()
                to_peer(shift).wait_send()
            mine.wait()

        return [begin, lambda: None, end]


def move_kernel(jobs, n_dp, n_ctx, n_others, *refs):
    at = Place(n_dp, n_ctx)
    operands, refs = refs[: len(jobs)], refs[len(jobs) + n_others :]
    outs, refs = refs[: len(jobs)], list(refs[len(jobs) :])
    lists = []
    for job, operand, out in zip(jobs, operands, outs):
        scratch = [refs.pop(0) for _ in job.scratch]
        lists.append(job.phases(at, operand, out, *scratch))
    at.meet(
        any(job.along_dp for job in jobs),
        any(job.along_ctx for job in jobs),
        any(job.across for job in jobs),
    )
    for phase in zip(*lists):
        for step in phase:
            step()


def move(collective_id, name, *kinds_and_values, others=()):
    n_dp, n_ctx = lax.axis_size("dp"), lax.axis_size("ctx")
    jobs = [kind(values, n_dp, n_ctx) for kind, values in kinds_and_values]
    values = [value for _, value in kinds_and_values]
    return pl.pallas_call(
        functools.partial(move_kernel, jobs, n_dp, n_ctx, len(others)),
        out_shape=[job.out_shape for job in jobs],
        in_specs=[job.operand_spec for job in jobs]
        + [pl.BlockSpec(memory_space=pl.ANY)] * len(others),
        out_specs=[job.out_spec for job in jobs],
        scratch_shapes=[piece for job in jobs for piece in job.scratch],
        compiler_params=pltpu.CompilerParams(
            collective_id=collective_id, has_side_effects=True, vmem_limit_bytes=58 * 2**20
        ),
        cost_estimate=pl.CostEstimate(flops=0, bytes_accessed=2**20, transcendentals=0),
        name=name,
    )(*values, *others)


def after(values, other):
    first = lax.slice(other.reshape(-1), (0,), (1,))[0]
    return jnp.where(first != first, jnp.zeros_like(values), values)


def pad_rows(values, rows):
    flat = values.reshape(-1)
    return jnp.pad(flat, (0, rows * 128 - flat.size)).reshape(rows, 128)


def pair_sum(blocks):
    while blocks.shape[0] > 1:
        blocks = blocks[0::2] + blocks[1::2]
    return blocks[0]


def body(
    tokens,
    output_grad,
    segment_ids,
    positions,
    qkv_weight,
    qkv_first,
    qkv_second,
    out_weight,
    out_first,
    out_second,
    gate_up_weight,
    gate_up_first,
    gate_up_second,
    down_weight,
    down_first,
    down_second,
    norm_gains,
    norm_first,
    norm_second,
    head_gains,
    head_first,
    head_second,
):
    n_dp, n_ctx = lax.axis_size("dp"), lax.axis_size("ctx")
    ctx_rank = lax.axis_index("ctx")
    seqs, length, width = tokens.shape
    own = norm_gains.shape[1]
    ff = down_weight.shape[0] * n_dp * n_ctx
    part = ff // n_dp

    kv_heads = KV // n_dp
    heads = kv_heads * G
    each = range(seqs)
    blocks = n_dp * seqs

    def spread_width(values):
        values = values.reshape(-1, n_dp, n_ctx, own).transpose(0, 2, 1, 3)
        return values.reshape(-1, width)

    def restore_width(values):
        values = values.reshape(-1, n_ctx, n_dp, own).transpose(0, 2, 1, 3)
        return values.reshape(-1, width)

    turned = jnp.arange(seqs, dtype=jnp.int32) % 2
    rank_of = ctx_rank + turned * (n_ctx - 1 - 2 * ctx_rank)
    places = jnp.stack([segment_ids, positions], axis=1)

    gain_one, gain_two = norm_gains[0][:, None], norm_gains[1][:, None]
    qkv_low = qkv_weight.astype(LOW).astype(F32)
    gate_up_low = gate_up_weight.astype(LOW).astype(F32)
    qkv_scaled = (qkv_low * gain_one).astype(LOW)
    qkv_blocks = jnp.concatenate(
        [
            block.reshape(own, n_dp, -1).transpose(1, 0, 2)
            for block in jnp.split(qkv_scaled, (H * HD, (H + KV) * HD), axis=1)
        ],
        axis=2,
    )
    qkv_cols = qkv_blocks.shape[2]

    def gather_ctx(values):
        return lax.all_gather(values.reshape(-1, values.shape[-1]), "ctx", axis=0, tiled=True)

    def scatter_ctx(values):
        return lax.psum_scatter(values, "ctx", scatter_dimension=0, tiled=True)

    qkv_mine, places_turned = move(
        1, "exchange_qkv", (ExchangeDp, qkv_blocks), (Mirror, pad_rows(places[1], 8))
    )
    qkv_part = gather_ctx(qkv_mine)
    down_part = gather_ctx(down_weight.astype(LOW))
    gate_up_blocks = (gate_up_low * gain_two).astype(LOW).reshape(own, 2, n_dp, part)
    gate_up_blocks = gate_up_blocks.transpose(2, 0, 1, 3).reshape(n_dp, own, 2 * part)
    places_turned = places_turned.reshape(-1)[: 2 * length].reshape(1, 2, length)
    places_of = jnp.concatenate([places[:1], places_turned], axis=0)

    def normed_rows(values):
        inputs = values.astype(F32)
        scale = rms_scale(inputs)
        return inputs, scale, spread_width((inputs * scale).astype(LOW))

    inputs_first, scale_first, normed = normed_rows(tokens[0])
    normed_first, tokens_turned, places_all = move(
        2,
        "gather_normed",
        (GatherDp, normed),
        (Mirror, tokens[1]),
        (GatherDp, pad_rows(places_of, 32)),
        others=(qkv_mine,),
    )
    inputs_second, scale_second, normed = normed_rows(tokens_turned)
    normed_second, grad_turned, gate_up_mine = move(
        3,
        "gather_normed",
        (GatherDp, normed),
        (Mirror, output_grad[1]),
        (ExchangeDp, gate_up_blocks),
    )
    inputs_of, scale_of = [inputs_first, inputs_second], [scale_first, scale_second]
    normed_of = [
        values.reshape(n_dp * length, width) for values in (normed_first, normed_second)
    ]
    projected_of = [
        dot(normed_of[s], qkv_part, NN).reshape(n_dp, length, qkv_cols) for s in each
    ]
    places_all = places_all.reshape(n_dp, -1)[:, : seqs * 2 * length].reshape(blocks, 2, length)

    projected = jnp.stack(projected_of, axis=1).reshape(blocks, length, qkv_cols)
    query_raw = projected[..., : heads * HD].reshape(blocks, length, heads, HD)
    keys_raw = projected[..., heads * HD : (heads + kv_heads) * HD]
    keys_raw = keys_raw.reshape(blocks, length, kv_heads, HD)
    values = projected[..., (heads + kv_heads) * HD :].astype(LOW)
    values = values.reshape(blocks, length, kv_heads, HD)
    segments, place_ids = places_all[:, 0], places_all[:, 1]
    cosine, sine = rotary_tables(place_ids)
    cosine, sine = cosine[:, :, None, :], sine[:, :, None, :]
    query_scale, keys_scale = rms_scale(query_raw), rms_scale(keys_raw)
    query_rot = rotary(query_raw * query_scale * head_gains[0], cosine, sine).astype(LOW)
    keys_rot = rotary(keys_raw * keys_scale * head_gains[1], cosine, sine).astype(LOW)
    kv = jnp.concatenate([keys_rot, values], axis=-1).transpose(0, 2, 1, 3)
    grads = jnp.concatenate([output_grad[0], grad_turned], axis=0)
    kv_all, grad_all = move(
        4,
        "gather_keys",
        (GatherCtx, kv.reshape(blocks * kv_heads * length, 2 * HD)),
        (GatherDp, grads),
        others=(down_part,),
    )
    out_part = gather_ctx(after(out_weight.astype(LOW), kv_all))
    gate_up_part = gather_ctx(after(gate_up_mine, kv_all))
    kv_all = kv_all.reshape(n_ctx, blocks, kv_heads, length, 2 * HD)
    grad_all = grad_all.reshape(blocks * length, width)
    query = query_rot * LOW(1.0 / math.sqrt(HD))
    query = query.reshape(blocks, length, kv_heads, G, HD).transpose(0, 2, 3, 1, 4)
    query = jnp.pad(query, ((0, 0),) * 4 + ((0, HD),))
    query = query.reshape(blocks, kv_heads, G * length, 2 * HD)
    place = jnp.tile(rank_of, n_dp)
    index = place[:, None] * length + jnp.arange(length, dtype=jnp.int32)
    start = jnp.where(segments == 0, 0, index - place_ids)
    full = jnp.minimum((jnp.max(start, axis=1) + length - 1) // length, place)
    low = jnp.minimum(jnp.min(start, axis=1) // length, full)
    meta = jnp.stack([place, low, full, jnp.tile(turned, n_dp)], axis=1)
    item = (
        meta,
        jnp.tile(start[:, None, :], (1, 1, G)),
        jnp.tile(index[:, None, :], (1, 1, G)),
        query,
        kv_all,
    )
    attended, log_total = attend(*item)
    attended = attended.reshape(blocks * length, heads * HD)

    def to_blocks(values):
        return values.astype(LOW).reshape(n_dp, -1, width)

    (mixed,) = move(5, "sum_mixed", (SumDp, to_blocks(dot(attended, out_part, NN))))
    inputs = jnp.concatenate(inputs_of, axis=0)
    middle = inputs + mixed
    scale_two = rms_scale(middle)
    (feed_all,) = move(
        6, "gather_feed", (GatherDp, spread_width((middle * scale_two).astype(LOW)))
    )
    feed_all = feed_all.reshape(blocks * length, width)

    gate = dot(feed_all, gate_up_part[:, :part], NN)
    up = dot(feed_all, gate_up_part[:, part:], NN)
    sigmoid_gate = jax.nn.sigmoid(gate)
    silu_gate = gate * sigmoid_gate
    hidden = (silu_gate * up).astype(LOW)
    d_hidden = dot(grad_all, down_part, NT)
    d_gate = d_hidden * up * sigmoid_gate * (1.0 + gate * (1.0 - sigmoid_gate))
    d_up = d_hidden * silu_gate
    d_gate_up = jnp.concatenate([d_gate.astype(LOW), d_up.astype(LOW)], axis=1)
    gate_up_sum = dot(feed_all, d_gate_up, TN).astype(LOW)
    down_sum = dot(hidden, grad_all, TN).astype(LOW)
    gate_up_grad = scatter_ctx(gate_up_sum)
    (d_feed,) = move(
        7,
        "sum_feed",
        (SumDp, to_blocks(dot(d_gate_up, gate_up_part, NT))),
        others=(gate_up_sum,),
    )
    d_middle = grads.astype(F32) + norm_back(restore_width(d_feed), middle, scale_two)
    d_middle_low = d_middle.astype(LOW)
    (d_middle_all,) = move(8, "gather_middle", (GatherDp, d_middle_low))
    down_scattered = scatter_ctx(after(after(down_sum, d_middle_all), gate_up_grad))
    d_middle_all = d_middle_all.reshape(blocks * length, width)

    d_attended = dot(d_middle_all, after(out_part, gate_up_grad), NT).astype(LOW)
    inner = (
        jnp.sum(
            (d_attended.astype(F32) * attended.astype(F32)).reshape(
                blocks, length, kv_heads, G, HD
            ),
            axis=-1,
        )
        .transpose(0, 2, 3, 1)
        .reshape(blocks, kv_heads, 1, G * length)
    )
    grad_items = d_attended.reshape(blocks, length, kv_heads, G, HD).transpose(0, 2, 3, 1, 4)
    grad_items = jnp.pad(grad_items, ((0, 0),) * 4 + ((HD, 0),))
    grad_items = grad_items.reshape(blocks, kv_heads, G * length, 2 * HD)
    d_query_rot, d_kv = attend_back(*item, grad_items, log_total, inner, gate_up_grad)
    out_sum = dot(attended, d_middle_all, TN).astype(LOW)
    out_grad = scatter_ctx(after(out_sum, down_scattered))
    d_kv, result, gate_up_grad = move(
        9,
        "sum_keys",
        (SumCtx, d_kv.reshape(n_ctx, blocks * kv_heads * length, 2 * HD)),
        (SumDp, to_blocks(dot(hidden, down_part, NN))),
        (ExchangeDp, gate_up_grad.reshape(n_dp, own, 2 * part)),
        others=(down_scattered,),
    )
    outputs = (middle + result).astype(LOW)
    d_kv = d_kv.reshape(blocks, kv_heads, length, 2 * HD).transpose(0, 2, 1, 3)
    d_query_rot = d_query_rot.reshape(blocks, length, heads, HD)
    d_query_norm = rotary_back(d_query_rot, cosine, sine)
    d_query = norm_back(d_query_norm * head_gains[0], query_raw, query_scale)
    d_keys_norm = rotary_back(d_kv[..., :HD], cosine, sine)
    d_keys = norm_back(d_keys_norm * head_gains[1], keys_raw, keys_scale)
    d_projected = jnp.concatenate(
        [
            d_query.astype(LOW).reshape(blocks, length, heads * HD),
            d_keys.astype(LOW).reshape(blocks, length, kv_heads * HD),
            d_kv[..., HD:].astype(LOW).reshape(blocks, length, kv_heads * HD),
        ],
        axis=2,
    ).reshape(n_dp, seqs, length, qkv_cols)
    head_terms = jnp.stack(
        [
            jnp.sum(d_query_norm * query_raw * query_scale, axis=(0, 1, 2)),
            jnp.sum(d_keys_norm * keys_raw * keys_scale, axis=(0, 1, 2)),
        ]
    )
    d_projected_of = [d_projected[:, s].reshape(n_dp * length, qkv_cols) for s in each]
    qkv_sum = sum(dot(normed_of[s], d_projected_of[s], TN) for s in each).astype(LOW)
    qkv_grad = scatter_ctx(qkv_sum)

    def input_gradient(seq, d_normed):
        d_inputs = norm_back(restore_width(d_normed), inputs_of[seq], scale_of[seq])
        return (d_middle[seq * length : (seq + 1) * length] + d_inputs).astype(LOW)

    d_normed, head_terms, outputs_second = move(
        10,
        "sum_normed",
        (SumDp, to_blocks(dot(d_projected_of[1], qkv_part, NT))),
        (GatherCtx, pad_rows(head_terms, 8)),
        (Mirror, outputs[length:]),
        others=(qkv_sum, out_grad),
    )
    head_terms = jnp.sum(head_terms, axis=0)
    d_normed, head_terms, input_grad_second, qkv_grad = move(
        11,
        "sum_normed",
        (SumDp, to_blocks(dot(d_projected_of[0], qkv_part, NT))),
        (GatherDp, pad_rows(head_terms, 32)),
        (Mirror, input_gradient(1, d_normed)),
        (ExchangeDp, qkv_grad.reshape(n_dp, own, qkv_cols)),
    )
    input_grad_first = input_gradient(0, d_normed)
    head_grad = pair_sum(head_terms)[:1].reshape(2, HD)
    qkv_grad = qkv_grad.astype(F32)
    qkv_grad = jnp.concatenate(
        [
            block.transpose(1, 0, 2).reshape(own, -1)
            for block in jnp.split(qkv_grad, (heads * HD, (heads + kv_heads) * HD), axis=2)
        ],
        axis=1,
    )
    out_grad = out_grad.astype(F32)
    down_grad = down_scattered.astype(F32)
    gate_up_grad = gate_up_grad.reshape(n_dp, own, 2, part).transpose(1, 2, 0, 3)
    gate_up_grad = gate_up_grad.reshape(own, 2 * ff).astype(F32)
    norm_grad = jnp.stack(
        [jnp.sum(qkv_low * qkv_grad, axis=1), jnp.sum(gate_up_low * gate_up_grad, axis=1)]
    )
    qkv_new = adam(qkv_weight, qkv_first, qkv_second, qkv_grad * gain_one, RATE_QKV, DECAY)
    out_new = adam(out_weight, out_first, out_second, out_grad, RATE_OUT, DECAY)
    gate_up_new = adam(
        gate_up_weight,
        gate_up_first,
        gate_up_second,
        gate_up_grad * gain_two,
        RATE_GATE_UP,
        DECAY,
    )
    down_new = adam(down_weight, down_first, down_second, down_grad, RATE_DOWN, DECAY)
    norm_new = adam(norm_gains, norm_first, norm_second, norm_grad, RATE_GAIN, 0.0)
    head_new = adam(head_gains, head_first, head_second, head_grad, RATE_GAIN, 0.0)
    return (
        jnp.stack([outputs[:length], outputs_second]),
        jnp.stack([input_grad_first, input_grad_second]),
        *qkv_new,
        *out_new,
        *gate_up_new,
        *down_new,
        *norm_new,
        *head_new,
    )


def solution(mesh):
    tokens_spec = P("dp", "ctx", None)
    matrix = P(("dp", "ctx"), None)
    gains = P(None, ("dp", "ctx"))
    in_specs = (
        (tokens_spec,) * 2 + (P("dp", "ctx"),) * 2 + (matrix,) * 12 + (gains,) * 3 + (P(),) * 3
    )
    out_specs = (tokens_spec,) * 2 + (matrix,) * 12 + (gains,) * 3 + (P(),) * 3
    return jax.shard_map(body, mesh=mesh, in_specs=in_specs, out_specs=out_specs, check_vma=False)
```

time: 1700 us -> 1540 us (0.906)
  Pallas kernels: 126 us -> 891 us
  waiting for transfers between devices: 666 us -> 37 us
  blocking collectives: 132 us -> 0 us
  matrix products: 357 us -> 275 us
  starting transfers between devices: 41.3 us -> 0.33 us
  other arithmetic: 128 us -> 104 us
    pallas_call x4 -> x13, Pallas kernels: 126 us -> 891 us  [the longest x11 796 us: move(): pl.pallas_call(functools.partial(move_kernel, jobs, n_dp, n_ctx, len(othe...]
    ppermute x35 -> x0, waiting for transfers between devices: 310 us -> none  [the longest x30 196 us: partners(): return lax.ppermute(values, axis, [(i, i ^ shift) for i in range(count)])]
    all_gather x6 -> x4, waiting for transfers between devices: 235 us -> 36.8 us  [gather_ctx(): lax.all_gather(values.reshape(-1, values.shape[-1]), 'ctx', axis=0, tiled...]
    psum x1 -> x0, blocking collectives: 132 us -> none  [body(): head_grad = lax.psum(sum(head_terms), everyone)]
    reduce_scatter x5 -> x4, waiting for transfers between devices: 121 us -> 0.05 us  [scatter_ctx(): return lax.psum_scatter(values, 'ctx', scatter_dimension=0, tiled=True)]
    dot_general x26 -> x16, matrix products: 357 us -> 275 us  [dot(): lax.dot_general(left, right, (dims, ((), ())), preferred_element_type=F32)]
    ppermute x35 -> x0, starting transfers between devices: 40.3 us -> none  [the longest x30 33.7 us: partners(): return lax.ppermute(values, axis, [(i, i ^ shift) for i in range(count)])]
    unnamed x272 -> x219, local copies, waits for them, and re-layouts: 30.5 us -> 47.1 us
  transfers between devices with their start and end apart: 46 -> 8, of which waited for: 21 -> 1; matrix products, arithmetic and copies ran while one was open for 38% -> 26% of each run, Pallas kernels for 3% -> 45%
where the time goes in v2:
time: 1540 us
  Pallas kernels  891 us (58%)
  matrix products  275 us (18%)
  local copies, waits for them, and re-layouts  208 us (14%)
  other arithmetic  104 us (7%)
  waiting for transfers between devices  37 us (2%)
  between operations  21.4 us (1%)
    pallas_call x11, Pallas kernels, move(): pl.pallas_call(functools.partial(move_kernel, jobs, n_dp, n_ctx, len(othe...  796 us
    dot_general x16, matrix products, dot(): lax.dot_general(left, right, (dims, ((), ())), preferred_element_type=F32)  275 us
    pallas_call x1, Pallas kernels, attend_back(): pl.pallas_call(attend_back_kernel, grid_spec=pltpu.PrefetchScalarGridSpec...  60.8 us
    unnamed x219, local copies, waits for them, and re-layouts  47.1 us
    all_gather x4, waiting for transfers between devices, gather_ctx(): lax.all_gather(values.reshape(-1, values.shape[-1]), 'ctx', axis=0, tiled...  36.8 us
    pallas_call x1, Pallas kernels, attend(): pl.pallas_call(attend_kernel, grid_spec=pltpu.PrefetchScalarGridSpec(num_...  34.7 us
  transfers between devices with their start and end apart: 8, of which 1 were waited for; matrix products, arithmetic and copies ran while one was open for 26% of the time, Pallas kernels for 45%

profile of v2, /device:TPU:0, one launch (start us, length us, event | category | flops | bytes accessed | tf_op | source)
XLA Modules:
  0.0 1536.9 jit_solution(5776829246834309971)
XLA Ops:
  11.7 13.1 exchange_qkv.1
  37.8 42.1 %gather_normed.2 = (bf16[4,256,2048]{2,1,0:T(8,128)(2,1)}, bf16[256,2048]{1,0:T(8,128)(2,1)}, s32[4,32,128]{2,1,0:T(8,128)}) custom-call(bf16[256,2048]{1,0:T(8,128)(2,1)} %copy.216.refs_0_, bf16[256,2048]{1,0:T(8,128)(2,1)} %get-tuple-element.118.refs_1_, s32[32,128]{1,0:T(8,128)} %pad_bitcast_fusion.1.refs_2_, bf16[4,64,768]{2,1,0:T(8,128)(2,1)} %get-tuple-element.45.refs_3_), custom_call_target="tpu_custom_call" | custom-call | bytes 1048576 | tf_op jit(solution)/shard_map/gather_normed/pallas_call | solution.py:696
  100.3 60.6 %gather_normed.3 = (bf16[4,256,2048]{2,1,0:T(8,128)(2,1)}, bf16[256,2048]{1,0:T(8,128)(2,1)}, bf16[4,64,4096]{2,1,0:T(8,128)(2,1)}) custom-call(bf16[256,2048]{1,0:T(8,128)(2,1)} %copy.233.refs_0_, bf16[256,2048]{1,0:T(8,128)(2,1)} %get-tuple-element.121.refs_1_, bf16[4,64,4096]{2,1,0:T(8,128)(2,1)} %reshape.595.refs_2_), custom_call_target="tpu_custom_call" | custom-call | bytes 1048576 | tf_op jit(solution)/shard_map/gather_normed/pallas_call | solution.py:696
  165.1 6.5 fusion.30
  182.6 36.8 %all-gather.7.cloned.1.call-done.refs_2_ = bf16[2048,2048]{1,0:T(8,128)(2,1)} async-done(((bf16[256,2048]{1,0:T(8,128)(2,1)}), bf16[2048,2048]{1,0:T(8,128)(2,1)}) %all-gather.7.cloned.1.call-update) | async-done | bytes 8388624 | tf_op jit(solution)/shard_map/all_gather | solution.py:789
  219.3 143.5 %gather_keys.1 = (bf16[8,4096,128]{2,1,0:T(8,128)(2,1)}, bf16[4,512,2048]{2,1,0:T(8,128)(2,1)}) custom-call(bf16[4096,128]{1,0:T(8,128)(2,1)} %bitcast.307, bf16[512,2048]{1,0:T(8,128)(2,1)} %pad_maximum_fusion.8.refs_1_, bf16[2048,2048]{1,0:T(8,128)(2,1)} %all-gather.7.cloned.1.call-done.refs_2_), custom_call_target="tpu_custom_call" | custom-call | bytes 1048576 | tf_op jit(solution)/shard_map/gather_keys/pallas_call | solution.py:696
  402.5 34.7 %attend.1 = (bf16[8,256,512]{2,1,0:T(8,128)(2,1)S(1)}, f32[8,2,1,1024]{3,2,1,0:T(1,128)S(1)}) custom-call(s32[8,4]{1,0:T(8,128)S(1)} %pad_add_fusion.1.meta_ref, s32[8,1,1024]{2,1,0:T(1,128)S(1)} %tile.35.start_ref, s32[8,1,1024]{2,1,0:T(1,128)S(1)} %tile.37.index_ref, bf16[8,2,1024,128]{3,2,1,0:T(8,128)(2,1)S(1)} %bitcast.243, ...), custom_call_target="tpu_custom_call" | custom-call | flops 1073741824 | bytes 1048576 | tf_op jit(solution)/shard_map/attend/pallas_call | solution.py:177
  437.3 20.4 %fusion.75 = f32[2048,2048]{0,1:T(8,128)} fusion(bf16[2048,2048]{1,0:T(8,128)(2,1)S(1)} %bitcast.343, bf16[2048,2048]{1,0:T(8,128)(2,1)S(1)} %bitcast.283), kind=kOutput, calls=%fused_computation.212 | convolution fusion | flops 17179869184 | bytes 33554432 | tf_op jit(solution)/shard_map/dot_general | solution.py:59
  457.8 8.5 convolution_convert_fusion.2
  466.3 71.7 %sum_mixed.1 = f32[512,2048]{1,0:T(8,128)} custom-call(bf16[4,512,2048]{2,1,0:T(8,128)(2,1)} %bitcast.281), custom_call_target="tpu_custom_call" | custom-call | bytes 1048576 | tf_op jit(solution)/shard_map/sum_mixed/pallas_call | solution.py:696
  552.5 66.4 %gather_feed.1 = bf16[4,512,2048]{2,1,0:T(8,128)(2,1)} custom-call(bf16[512,2048]{1,0:T(8,128)(2,1)} %copy.243.refs_0_), custom_call_target="tpu_custom_call" | custom-call | bytes 1048576 | tf_op jit(solution)/shard_map/gather_feed/pallas_call | solution.py:696
  618.9 24.3 %fusion.2 = f32[2048,2048]{0,1:T(8,128)} fusion(bf16[2048,2048]{1,0:T(8,128)(2,1)} %bitcast.277, bf16[2048,4096]{1,0:T(8,128)(2,1)} %all-gather.11.cloned.1.call-done), kind=kOutput, calls=%fused_computation.8 | convolution fusion | flops 17179869184 | bytes 33554432 | tf_op jit(solution)/shard_map/dot_general | solution.py:59
  643.2 36.5 %multiply_convert_fusion = (bf16[2048,2048]{0,1:T(8,128)(2,1)}, bf16[2048,2048]{0,1:T(8,128)(2,1)}, bf16[2048,2048]{0,1:T(8,128)(2,1)}) fusion(f32[2048,2048]{0,1:T(8,128)} %fusion.2, f32[2048,2048]{0,1:T(8,128)} %fusion.75, bf16[2048,2048]{1,0:T(8,128)(2,1)} %bitcast.278, bf16[2048,4096]{1,0:T(8,128)(2,1)} %all-gather.11.cloned.1.call-done), kind=kOutput, calls=%fused_computation.1 | convolution fusion | flops 17242783744 | bytes 75497472 | tf_op jit(solution)/shard_map/dot_general | solution.py:59
  679.8 43.2 %convolution_convert_fusion.refs_1_ = bf16[2048,4096]{1,0:T(8,128)(2,1)} fusion(bf16[2048,2048]{1,0:T(8,128)(2,1)} %bitcast.279, bf16[2048,2048]{0,1:T(8,128)(2,1)} %get-tuple-element.99, bf16[2048,2048]{0,1:T(8,128)(2,1)} %get-tuple-element.98), kind=kOutput, calls=%fused_computation.6 | convolution fusion | flops 34401681408 | bytes 41943040 | tf_op jit(solution)/shard_map/dot_general | solution.py:59
  723.1 44.5 %fusion.6 = bf16[2048,2048]{1,0:T(8,128)(2,1)} fusion(bf16[2048,4096]{1,0:T(8,128)(2,1)} %all-gather.11.cloned.1.call-done, bf16[2048,2048]{0,1:T(8,128)(2,1)} %get-tuple-element.99, bf16[2048,2048]{0,1:T(8,128)(2,1)} %get-tuple-element.98), kind=kOutput, calls=%fused_computation.15 | convolution fusion | flops 34397487104 | bytes 41943040 | tf_op jit(solution)/shard_map/dot_general | solution.py:59
  767.6 69.6 %sum_feed.1 = f32[512,2048]{1,0:T(8,128)} custom-call(bf16[4,512,2048]{2,1,0:T(8,128)(2,1)} %bitcast.275, bf16[2048,4096]{1,0:T(8,128)(2,1)} %convolution_convert_fusion.refs_1_), custom_call_target="tpu_custom_call" | custom-call | bytes 1048576 | tf_op jit(solution)/shard_map/sum_feed/pallas_call | solution.py:696
  863.8 66.7 %gather_middle.1 = bf16[4,512,2048]{2,1,0:T(8,128)(2,1)} custom-call(bf16[512,2048]{1,0:T(8,128)(2,1)} %get-tuple-element.88.refs_0_), custom_call_target="tpu_custom_call" | custom-call | bytes 1048576 | tf_op jit(solution)/shard_map/gather_middle/pallas_call | solution.py:696
  930.5 9.9 copy.294
  946.8 23.7 %select_select_fusion = bf16[2048,2048]{1,0:T(8,128)(2,1)} fusion(pred[]{:T(512)} %bitcast.65, pred[]{:T(512)} %bitcast.58, bf16[2048,2048]{0,1:T(8,128)(2,1)} %get-tuple-element.97, bf16[2048,2048]{1,0:T(8,128)(2,1)} %bitcast.340), kind=kOutput, calls=%fused_computation.12 | convolution fusion | flops 17192452096 | bytes 25165826 | tf_op jit(solution)/shard_map/dot_general | solution.py:59
  980.6 23.9 %convolution_convert_fusion.1 = bf16[2048,2048]{1,0:T(8,128)(2,1)} fusion(bf16[2048,2048]{0,1:T(8,128)(2,1)} %get-tuple-element.97, bf16[2048,2048]{1,0:T(8,128)(2,1)} %all-gather.7.cloned.1.call-done.refs_2_), kind=kOutput, calls=%fused_computation.13 | convolution fusion | flops 17184063488 | bytes 25165824 | tf_op jit(solution)/shard_map/dot_general | solution.py:59
  1004.6 9.7 convert_multiply_fusion.2
  1033.9 6.2 copy.293
  1045.3 60.8 %attend_back.1 = (f32[8,256,512]{2,1,0:T(8,128)S(1)}, bf16[8,8,2,256,128]{4,3,2,1,0:T(8,128)(2,1)}) custom-call(s32[8,4]{1,0:T(8,128)S(1)} %copy-done.9, s32[8,1,1024]{2,1,0:T(1,128)S(1)} %copy-done.5, s32[8,1,1024]{2,1,0:T(1,128)S(1)} %copy-done.7, bf16[8,2,1024,128]{3,2,1,0:T(8,128)(2,1)S(1)} %bitcast.244, bf16[8,8,2,256,128]{4,3,2,1,0:T(8,128)(2,1)} %bitcast.259, ...), custom_call_target="tpu_custom_call" | custom-call | flops 2147483648 | bytes 1048576 | tf_op jit(solution)/shard_map/attend_back/pallas_call | solution.py:202
  1133.2 8.1 multiply_reduce_fusion
  1144.8 9.3 fusion.19
  1154.1 136.5 %sum_keys.1 = (f32[4096,128]{1,0:T(8,128)}, f32[512,2048]{1,0:T(8,128)}, bf16[4,64,4096]{2,1,0:T(8,128)(2,1)}) custom-call(bf16[8,4096,128]{2,1,0:T(8,128)(2,1)} %bitcast.285, bf16[4,512,2048]{2,1,0:T(8,128)(2,1)} %bitcast.284, bf16[4,64,4096]{2,1,0:T(8,128)(2,1)} %bitcast.246, bf16[256,2048]{1,0:T(8,128)(2,1)} %reduce-scatter.7.cloned.1.call-done.refs_3_), custom_call_target="tpu_custom_call" | custom-call | bytes 1048576 | tf_op jit(solution)/shard_map/sum_keys/pallas_call | solution.py:696
  1323.9 6.8 reshape.647
  1330.6 8.1 copy.279
  1338.8 6.1 reshape.646
  1346.9 7.2 convolution_convert_fusion.4
  1372.5 78.1 %sum_normed.2 = (f32[256,2048]{1,0:T(8,128)}, f32[8,8,128]{2,1,0:T(8,128)}, bf16[256,2048]{1,0:T(8,128)(2,1)}) custom-call(bf16[4,256,2048]{2,1,0:T(8,128)(2,1)} %bitcast.306, f32[8,128]{1,0:T(8,128)} %pad_bitcast_fusion.2.refs_1_, bf16[256,2048]{1,0:T(8,128)(2,1)} %get-tuple-element.116.refs_2_, bf16[2048,768]{1,0:T(8,128)(2,1)} %add_convert_fusion.refs_3_, ...), custom_call_target="tpu_custom_call" | custom-call | bytes 1048576 | tf_op jit(solution)/shard_map/sum_normed/pallas_call | solution.py:696
  1463.2 47.3 %sum_normed.3 = (f32[256,2048]{1,0:T(8,128)}, f32[4,32,128]{2,1,0:T(8,128)}, bf16[256,2048]{1,0:T(8,128)(2,1)}, bf16[4,64,768]{2,1,0:T(8,128)(2,1)}) custom-call(bf16[4,256,2048]{2,1,0:T(8,128)(2,1)} %bitcast.297, f32[32,128]{1,0:T(8,128)} %pad_bitcast_fusion.refs_1_, bf16[256,2048]{1,0:T(8,128)(2,1)} %fusion.22.refs_2_, bf16[4,64,768]{2,1,0:T(8,128)(2,1)} %bitcast.324), custom_call_target="tpu_custom_call" | custom-call | bytes 1048576 | tf_op jit(solution)/shard_map/sum_normed/pallas_call | solution.py:696
  (415 shorter events, 284.6 us)
Async XLA Ops:
  7.2 157.9 %all-gather.5.cloned.1.call-start = ((), (), s32[]{:S(2)}) async-start(), calls=%async_computation.4 | async-start | bytes 3538944 | tf_op jit(solution)/shard_map/all_gather | solution.py:789
  8.0 77.5 %copy-start.81 = (f32[64]{0:T(128)}, f32[64]{0:T(128)S(1)}, u32[]{:S(2)}) copy-start(f32[64]{0:T(128)S(1)} %get-tuple-element.141) | copy-start | bytes 772
  8.0 19.7 %copy-start.34 = (bf16[2,256,2048]{2,1,0:T(8,128)(2,1)S(1)}, bf16[2,256,2048]{2,1,0:T(8,128)(2,1)}, u32[]{:S(2)}) copy-start(bf16[2,256,2048]{2,1,0:T(8,128)(2,1)} %param.22) | copy-start | bytes 6291460
  24.8 194.5 %all-gather.7.cloned.1.call-start = ((), (), s32[]{:S(2)}) async-start(), calls=%async_computation.5 | async-start | bytes 9437184 | tf_op jit(solution)/shard_map/all_gather | solution.py:789
  27.6 430.2 %all-gather.9.cloned.1.call-start = ((), (), s32[]{:S(2)}) async-start(), calls=%async_computation.6 | async-start | bytes 2359296 | tf_op jit(solution)/shard_map/all_gather | solution.py:789
  97.5 63.4 %copy-start.85 = (f32[2,64]{1,0:T(2,128)S(1)}, f32[2,64]{1,0:T(2,128)}, u32[]{:S(2)}) copy-start(f32[2,64]{1,0:T(2,128)} %param.41) | copy-start | bytes 1540
  100.3 61.8 %copy-start.30 = (bf16[256,2048]{1,0:T(8,128)(2,1)}, bf16[256,2048]{1,0:T(8,128)(2,1)S(1)}, u32[]{:S(2)}) copy-start(bf16[256,2048]{1,0:T(8,128)(2,1)S(1)} %get-tuple-element.120) | copy-start | bytes 3145732
  160.9 19.3 %copy-start.83 = (f32[64]{0:T(128)}, f32[64]{0:T(128)S(1)}, u32[]{:S(2)}) copy-start(f32[64]{0:T(128)S(1)} %get-tuple-element.139) | copy-start | bytes 772
  161.0 224.5 %copy-start.77 = (f32[64]{0:T(128)}, f32[64]{0:T(128)S(1)}, u32[]{:S(2)}) copy-start(f32[64]{0:T(128)S(1)} %get-tuple-element.140) | copy-start | bytes 772
  162.0 224.9 %copy-start.39 = (f32[8,256,32]{1,2,0:T(8,128)}, f32[8,256,32]{1,2,0:T(8,128)S(1)}, u32[]{:S(2)}) copy-start(f32[8,256,32]{1,2,0:T(8,128)S(1)} %get-tuple-element.135) | copy-start | bytes 786436
  162.0 224.9 %copy-start.41 = (f32[8,256,32]{1,2,0:T(8,128)}, f32[8,256,32]{1,2,0:T(8,128)S(1)}, u32[]{:S(2)}) copy-start(f32[8,256,32]{1,2,0:T(8,128)S(1)} %get-tuple-element.136) | copy-start | bytes 786436
  219.3 146.1 %copy-start.49 = (f32[64,2048]{1,0:T(8,128)S(1)}, f32[64,2048]{1,0:T(8,128)}, u32[]{:S(2)}) copy-start(f32[64,2048]{1,0:T(8,128)} %param.29) | copy-start | bytes 1572868
  366.2 252.7 %all-gather.11.cloned.1.call-start = ((), (), s32[]{:S(2)}) async-start(), calls=%async_computation.7 | async-start | bytes 18874368 | tf_op jit(solution)/shard_map/all_gather | solution.py:789
  369.4 573.5 %reduce-scatter.5.cloned.1.call-start = ((), (), s32[]{:S(2)}) async-start(), calls=%async_computation.8 | async-start | bytes 18874368 | tf_op jit(solution)/shard_map/reduce_scatter | solution.py:792
  371.7 30.8 %copy-start.4 = (s32[8,1,1024]{2,1,0:T(1,128)}, s32[8,1,1024]{2,1,0:T(1,128)S(1)}, u32[]{:S(2)}) copy-start(s32[8,1,1024]{2,1,0:T(1,128)S(1)} %tile.35.start_ref) | copy-start | bytes 98308
  371.8 30.7 %copy-start.6 = (s32[8,1,1024]{2,1,0:T(1,128)}, s32[8,1,1024]{2,1,0:T(1,128)S(1)}, u32[]{:S(2)}) copy-start(s32[8,1,1024]{2,1,0:T(1,128)S(1)} %tile.37.index_ref) | copy-start | bytes 98308
  371.9 30.6 %copy-start.8 = (s32[8,4]{1,0:T(8,128)}, s32[8,4]{1,0:T(8,128)S(1)}, u32[]{:S(2)}) copy-start(s32[8,4]{1,0:T(8,128)S(1)} %pad_add_fusion.1.meta_ref) | copy-start | bytes 388
  396.3 41.0 %slice-start.2 = ((s8[8388608]{0:T(1024)(128)(4,1)}), s8[4194304]{0:T(1024)(128)(4,1)S(1)}, s32[]{:S(2)}) async-start(s8[8388608]{0:T(1024)(128)(4,1)} %bitcast.341), calls=%async_computation.14 | async-start | bytes 8388608
  401.3 36.0 %slice-start = ((s8[8388608]{0:T(1024)(128)(4,1)}), s8[4194304]{0:T(1024)(128)(4,1)S(1)}, s32[]{:S(2)}) async-start(s8[8388608]{0:T(1024)(128)(4,1)} %bitcast.282), calls=%async_computation.12 | async-start | bytes 8388608
  401.3 36.0 %slice-start.3 = ((s8[8388608]{0:T(1024)(128)(4,1)}), s8[4194304]{0:T(1024)(128)(4,1)S(1)}, s32[]{:S(2)}) async-start(s8[8388608]{0:T(1024)(128)(4,1)} %bitcast.341), calls=%async_computation.15 | async-start | bytes 8388608
  402.4 34.8 %copy-start = (bf16[8,2,4,256,128]{4,3,2,1,0:T(8,128)(2,1)}, bf16[8,2,4,256,128]{4,3,2,1,0:T(8,128)(2,1)S(1)}, u32[]{:S(2)}) copy-start(bf16[8,2,4,256,128]{4,3,2,1,0:T(8,128)(2,1)S(1)} %pad.26) | copy-start | bytes 12582916
  402.5 34.8 %slice-start.1 = ((s8[8388608]{0:T(1024)(128)(4,1)}), s8[4194304]{0:T(1024)(128)(4,1)S(1)}, s32[]{:S(2)}) async-start(s8[8388608]{0:T(1024)(128)(4,1)} %bitcast.282), calls=%async_computation.13 | async-start | bytes 8388608
  437.3 20.5 %copy-start.10 = (bf16[8,256,512]{2,1,0:T(8,128)(2,1)}, bf16[8,256,512]{2,1,0:T(8,128)(2,1)S(1)}, u32[]{:S(2)}) copy-start(bf16[8,256,512]{2,1,0:T(8,128)(2,1)S(1)} %get-tuple-element.52) | copy-start | bytes 6291460
  466.3 71.7 %copy-start.36 = (f32[256,2048]{1,0:T(8,128)S(1)}, f32[256,2048]{1,0:T(8,128)}, u32[]{:S(2)}) copy-start(f32[256,2048]{1,0:T(8,128)} %get-tuple-element.117) | copy-start | bytes 6291460
  466.3 71.7 %copy-start.38 = (f32[256,2048]{1,0:T(8,128)S(1)}, f32[256,2048]{1,0:T(8,128)}, u32[]{:S(2)}) copy-start(f32[256,2048]{1,0:T(8,128)} %convert_element_type.174) | copy-start | bytes 6291460
  723.0 418.5 %reduce-scatter.7.cloned.1.call-start = ((), (), s32[]{:S(2)}) async-start(), calls=%async_computation.9 | async-start | bytes 9437184 | tf_op jit(solution)/shard_map/reduce_scatter | solution.py:792
  847.4 9.7 copy-start.45
  970.5 402.0 %reduce-scatter.9.cloned.1.call-start = ((), (), s32[]{:S(2)}) async-start(), calls=%async_computation.10 | async-start | bytes 2359296 | tf_op jit(solution)/shard_map/reduce_scatter | solution.py:792
  980.6 24.0 %copy-start.11 = (bf16[8,256,512]{2,1,0:T(8,128)(2,1)S(1)}, bf16[8,256,512]{2,1,0:T(8,128)(2,1)}, u32[]{:S(2)}) copy-start(bf16[8,256,512]{2,1,0:T(8,128)(2,1)} %copy-done.10) | copy-start | bytes 6291460
  980.6 24.0 %copy-start.98 = (bf16[512,2048]{1,0:T(8,128)(2,1)S(1)}, bf16[512,2048]{1,0:T(8,128)(2,1)}, u32[]{:S(2)}) copy-start(bf16[512,2048]{1,0:T(8,128)(2,1)} %all-gather.9.cloned.1.call-done) | copy-start | bytes 6291460
  1133.2 11.5 copy-start.12
  1154.1 309.1 %reduce-scatter.11.cloned.1.call-start = ((), (), s32[]{:S(2)}) async-start(), calls=%async_computation.11 | async-start | bytes 3538944 | tf_op jit(solution)/shard_map/reduce_scatter | solution.py:792
  (79 other events, 335.3 us)
Sparse Core Ops, SparseCore 0:
  24.9 67.9 all-gather.4
  95.1 124.2 all-gather.6
  366.4 27.2 all-gather.8
  395.7 150.5 all-gather.10
  723.1 177.7 reduce-scatter.4
  970.6 103.6 reduce-scatter.6
  1154.2 78.4 reduce-scatter.8
  1323.9 59.3 reduce-scatter.10

commit v3 on v2

--- a/solution.py
+++ b/solution.py
@@ -95,18 +95,28 @@
     step(place, True)
 
 
-def attend_kernel(meta_ref, start_ref, index_ref, query_ref, kv_ref, out_ref, log_ref, acc_ref):
-    length = query_ref.shape[2] // G
+def pad_heads(rows_ref, values_ref, side):
+    length = values_ref.shape[1]
+    zeros = jnp.zeros((length, HD), rows_ref.dtype)
+    for head in range(G):
+        values = values_ref[0, :, head * HD : (head + 1) * HD]
+        pair = [zeros, values] if side else [values, zeros]
+        rows_ref[pl.ds(head * length, length), :] = jnp.concatenate(pair, axis=1)
+
+
+def attend_kernel(meta_ref, start_ref, index_ref, query_ref, kv_ref, out_ref, log_ref, acc_ref, rows_ref):
+    length = query_ref.shape[1]
     start, query_index = start_ref[0], index_ref[0]
     turned = meta_ref[pl.program_id(0), 3]
     lane = lax.broadcasted_iota(jnp.int32, (length, 2 * HD), 1)
     acc_ref[...] = jnp.zeros_like(acc_ref)
+    pad_heads(rows_ref, query_ref, 0)
 
     def step(chunk, masked):
         slot = chunk + turned * (kv_ref.shape[0] - 1 - 2 * chunk)
         kv = kv_ref[slot, 0, 0]
         ones_v = jnp.where(lane < HD, jnp.ones_like(kv), kv)
-        probs = jnp.exp(dot(kv, query_ref[0, 0], NT))
+        probs = jnp.exp(dot(kv, rows_ref[...], NT))
         if masked:
             probs = jnp.where(chunk_mask(chunk, length, start, query_index), probs, 0.0)
         acc_ref[...] += dot(ones_v, probs.astype(LOW), TN)
@@ -132,12 +142,16 @@
     dq_ref,
     dkv_ref,
     acc_ref,
+    rows_ref,
+    grad_rows_ref,
 ):
-    length = query_ref.shape[2] // G
+    length = query_ref.shape[1]
     start, query_index = start_ref[0], index_ref[0]
     turned = meta_ref[pl.program_id(0), 3]
     acc_ref[...] = jnp.zeros_like(acc_ref)
     dkv_ref[...] = jnp.zeros_like(dkv_ref)
+    pad_heads(rows_ref, query_ref, 0)
+    pad_heads(grad_rows_ref, grad_ref, 1)
 
     def step(chunk, masked):
         slot = chunk + turned * (kv_ref.shape[0] - 1 - 2 * chunk)
@@ -145,7 +159,7 @@
         total = jnp.zeros((length, 2 * HD), F32)
         for head in range(G):
             part = pl.ds(head * length, length)
-            query, grad = query_ref[0, 0, part], grad_ref[0, 0, part]
+            query, grad = rows_ref[part], grad_rows_ref[part]
             probs = jnp.exp(dot(kv, query, NT) - log_ref[0, 0, :, part])
             if masked:
                 mask = chunk_mask(chunk, length, start[:, :length], query_index[:, :length])
@@ -162,26 +176,28 @@
 
 
 def attention_specs(n_ctx, length):
-    query = pl.BlockSpec((1, 1, G * length, 2 * HD), lambda b, h, *_: (b, h, 0, 0))
     kv = pl.BlockSpec((n_ctx, 1, 1, length, 2 * HD), lambda b, h, *_: (0, b, h, 0, 0))
     row = pl.BlockSpec((1, 1, 1, G * length), lambda b, h, *_: (b, h, 0, 0))
     start = pl.BlockSpec((1, 1, G * length), lambda b, h, *_: (b, 0, 0))
     natural = pl.BlockSpec((1, length, G * HD), lambda b, h, *_: (b, 0, h))
-    return query, kv, row, start, natural
+    return kv, row, start, natural
 
 
 def attend(meta, start, index, query, kv_all):
     n_ctx, blocks, heads, length, _ = kv_all.shape
-    q_spec, kv_spec, row_spec, start_spec, natural = attention_specs(n_ctx, length)
+    kv_spec, row_spec, start_spec, natural = attention_specs(n_ctx, length)
     pairs = blocks * heads * G * length * n_ctx * length
     return pl.pallas_call(
         attend_kernel,
         grid_spec=pltpu.PrefetchScalarGridSpec(
             num_scalar_prefetch=1,
             grid=(blocks, heads),
-            in_specs=[start_spec, start_spec, q_spec, kv_spec],
+            in_specs=[start_spec, start_spec, natural, kv_spec],
             out_specs=[natural, row_spec],
-            scratch_shapes=[pltpu.VMEM((2 * HD, G * length), F32)],
+            scratch_shapes=[
+                pltpu.VMEM((2 * HD, G * length), F32),
+                pltpu.VMEM((G * length, 2 * HD), LOW),
+            ],
         ),
         out_shape=[
             jax.ShapeDtypeStruct((blocks, length, heads * G * HD), LOW),
@@ -197,17 +213,21 @@
 
 def attend_back(meta, start, index, query, kv_all, grad, log_total, inner, other):
     n_ctx, blocks, heads, length, _ = kv_all.shape
-    q_spec, kv_spec, row_spec, start_spec, natural = attention_specs(n_ctx, length)
+    kv_spec, row_spec, start_spec, natural = attention_specs(n_ctx, length)
     pairs = blocks * heads * G * length * n_ctx * length
     return pl.pallas_call(
         attend_back_kernel,
         grid_spec=pltpu.PrefetchScalarGridSpec(
             num_scalar_prefetch=1,
             grid=(blocks, heads),
-            in_specs=[start_spec, start_spec, q_spec, kv_spec, q_spec, row_spec, row_spec]
+            in_specs=[start_spec, start_spec, natural, kv_spec, natural, row_spec, row_spec]
             + [pl.BlockSpec(memory_space=pl.ANY)],
             out_specs=[natural, kv_spec],
-            scratch_shapes=[pltpu.VMEM((2 * HD, G * length), F32)],
+            scratch_shapes=[
+                pltpu.VMEM((2 * HD, G * length), F32),
+                pltpu.VMEM((G * length, 2 * HD), LOW),
+                pltpu.VMEM((G * length, 2 * HD), LOW),
+            ],
         ),
         out_shape=[
             jax.ShapeDtypeStruct((blocks, length, heads * G * HD), F32),
@@ -329,12 +349,11 @@
                     straight(shift, chunk).start()
             mine.start()
 
-        def middle():
-            for chunk in range(CHUNKS):
-                for shift in direct:
-                    straight(shift, chunk).wait_recv()
-                    if halves:
-                        turned(3 - shift, chunk).start()
+        def middle(chunk):
+            for shift in direct:
+                straight(shift, chunk).wait_recv()
+                if halves:
+                    turned(3 - shift, chunk).start()
 
         def end():
             for chunk in range(CHUNKS):
@@ -345,7 +364,7 @@
                     straight(shift, chunk).wait_send()
             mine.wait()
 
-        return [begin, middle, end]
+        return begin, [functools.partial(middle, chunk) for chunk in range(CHUNKS)], end
 
 
 class SumDp:
@@ -408,16 +427,14 @@
                         if not halves or which != 2 - shift:
                             final(shift, chunk, which).start()
 
-        def middle():
-            if halves:
-                for chunk in range(CHUNKS):
-                    for shift in direct:
-                        turning(shift, chunk).wait_recv()
-                        to = 3 - shift
-                        mine = parts[to, rows(chunk, shift - 1)].astype(F32)
-                        came = arrived[shift - 1, chunk].astype(F32)
-                        joined[to - 1, chunk] = (mine + came).astype(LOW)
-                        final(to, chunk, shift - 1).start()
+        def middle(chunk):
+            for shift in direct if halves else ():
+                turning(shift, chunk).wait_recv()
+                to = 3 - shift
+                mine = parts[to, rows(chunk, shift - 1)].astype(F32)
+                came = arrived[shift - 1, chunk].astype(F32)
+                joined[to - 1, chunk] = (mine + came).astype(LOW)
+                final(to, chunk, shift - 1).start()
 
         def end():
             for chunk in range(CHUNKS):
@@ -434,7 +451,7 @@
                     for which in (0, 1):
                         final(shift, chunk, which).wait_send()
 
-        return [begin, middle, end]
+        return begin, [functools.partial(middle, chunk) for chunk in range(CHUNKS)], end
 
 
 class GatherCtx:
@@ -477,16 +494,14 @@
             mine.wait()
             pass_on(at.column)
 
-        def middle():
-            @pl.loop(1, 2 * at.last + 1)
-            def _(count):
-                away = (count + 1) // 2
-                column = at.column + away - 2 * away * (count % 2)
-
-                @pl.when((column >= 0) & (column <= at.last))
-                def _():
-                    travel(column, up_send, at.sibling).wait_recv()
-                    pass_on(column)
+        def middle(step):
+            def arrive(column):
+                travel(column, up_send, at.sibling).wait_recv()
+                pass_on(column)
+
+            low, high = at.column - step - 1, at.column + step + 1
+            pl.when(low >= 0)(lambda: arrive(low))
+            pl.when(high <= at.last)(lambda: arrive(high))
 
         def end():
             @pl.loop(0, at.last + 1)
@@ -500,7 +515,7 @@
                     lambda: travel(column, down_send, at.below).wait_send()
                 )
 
-        return [begin, middle, end]
+        return begin, [functools.partial(middle, step) for step in range(at.last)], end
 
 
 class SumCtx:
@@ -558,14 +573,12 @@
                 at.below,
             )
 
-        def farthest_first(step):
-            @pl.loop(0, at.last + 1)
-            def _(count):
-                odd = count % 2
-                step((1 - odd) * (at.last - count // 2) + odd * (count // 2))
+        def farthest_first(count):
+            return count // 2 if count % 2 else at.last - count // 2
 
         def begin():
-            farthest_first(lambda column: to_sibling(column).start())
+            for count in range(at.last + 1):
+                to_sibling(farthest_first(count)).start()
 
         def line(column):
             to_sibling(column).wait_recv()
@@ -593,8 +606,8 @@
 
                 to_below(column).start()
 
-        def middle():
-            farthest_first(line)
+        def middle(count):
+            line(farthest_first(count))
 
         def end():
             out[...] = acc[at.column].astype(F32)
@@ -615,7 +628,7 @@
                 pl.when(column > at.column)(lambda: to_above(column).wait_send())
                 pl.when(column < at.column)(lambda: to_below(column).wait_send())
 
-        return [begin, middle, end]
+        return begin, [functools.partial(middle, step) for step in range(at.last + 1)], end
 
 
 class Mirror:
@@ -629,7 +642,7 @@
 
     def phases(self, at, own, out, send, recv):
         copy = remote(own, out, send, recv, at.opposite)
-        return [copy.start, lambda: None, copy.wait]
+        return copy.start, [], copy.wait
 
 
 class ExchangeDp:
@@ -668,7 +681,7 @@
                 to_peer(shift).wait_send()
             mine.wait()
 
-        return [begin, lambda: None, end]
+        return begin, [], end
 
 
 def move_kernel(jobs, n_dp, n_ctx, n_others, *refs):
@@ -684,9 +697,14 @@
         any(job.along_ctx for job in jobs),
         any(job.across for job in jobs),
     )
-    for phase in zip(*lists):
-        for step in phase:
-            step()
+    for begin, _, _ in lists:
+        begin()
+    for count in range(max(len(middles) for _, middles, _ in lists)):
+        for _, middles, _ in lists:
+            if count < len(middles):
+                middles[count]()
+    for _, _, end in lists:
+        end()
 
 
 def move(collective_id, name, *kinds_and_values, others=()):
@@ -858,9 +876,7 @@
     kv_all = kv_all.reshape(n_ctx, blocks, kv_heads, length, 2 * HD)
     grad_all = grad_all.reshape(blocks * length, width)
     query = query_rot * LOW(1.0 / math.sqrt(HD))
-    query = query.reshape(blocks, length, kv_heads, G, HD).transpose(0, 2, 3, 1, 4)
-    query = jnp.pad(query, ((0, 0),) * 4 + ((0, HD),))
-    query = query.reshape(blocks, kv_heads, G * length, 2 * HD)
+    query = query.reshape(blocks, length, heads * HD)
     place = jnp.tile(rank_of, n_dp)
     index = place[:, None] * length + jnp.arange(length, dtype=jnp.int32)
     start = jnp.where(segments == 0, 0, index - place_ids)
@@ -924,17 +940,15 @@
         .transpose(0, 2, 3, 1)
         .reshape(blocks, kv_heads, 1, G * length)
     )
-    grad_items = d_attended.reshape(blocks, length, kv_heads, G, HD).transpose(0, 2, 3, 1, 4)
-    grad_items = jnp.pad(grad_items, ((0, 0),) * 4 + ((HD, 0),))
-    grad_items = grad_items.reshape(blocks, kv_heads, G * length, 2 * HD)
+    grad_items = d_attended.reshape(blocks, length, heads * HD)
     d_query_rot, d_kv = attend_back(*item, grad_items, log_total, inner, gate_up_grad)
     out_sum = dot(attended, d_middle_all, TN).astype(LOW)
     out_grad = scatter_ctx(after(out_sum, down_scattered))
-    d_kv, result, gate_up_grad = move(
+    result, d_kv, gate_up_grad = move(
         9,
         "sum_keys",
+        (SumDp, to_blocks(dot(hidden, down_part, NN))),
         (SumCtx, d_kv.reshape(n_ctx, blocks * kv_heads * length, 2 * HD)),
-        (SumDp, to_blocks(dot(hidden, down_part, NN))),
         (ExchangeDp, gate_up_grad.reshape(n_dp, own, 2 * part)),
         others=(down_scattered,),
     )

time: 1540 us -> 1510 us (0.981)
  Pallas kernels: 891 us -> 867 us
    pallas_call x11, Pallas kernels: 796 us -> 760 us  [move(): pl.pallas_call(functools.partial(move_kernel, jobs, n_dp, n_ctx, len(othe...]
    unnamed x219 -> x207, local copies, waits for them, and re-layouts: 47.1 us -> 47.8 us
  transfers between devices with their start and end apart: 8 -> 8, of which waited for: 1 -> 1; matrix products, arithmetic and copies ran while one was open for 26% -> 25% of each run, Pallas kernels for 45% -> 45%
where the time goes in v3:
time: 1510 us; the launch traced here: 1500 us
  Pallas kernels  867 us (57%)
  matrix products  280 us (19%)
  local copies, waits for them, and re-layouts  194 us (13%)
  other arithmetic  100 us (7%)
  waiting for transfers between devices  37 us (2%)
  between operations  21.3 us (1%)
    pallas_call x11, Pallas kernels, move(): pl.pallas_call(functools.partial(move_kernel, jobs, n_dp, n_ctx, len(othe...  760 us
    dot_general x16, matrix products, dot(): lax.dot_general(left, right, (dims, ((), ())), preferred_element_type=F32)  280 us
    pallas_call x1, Pallas kernels, attend_back(): pl.pallas_call(attend_back_kernel, grid_spec=pltpu.PrefetchScalarGridSpec...  72.8 us
    unnamed x207, local copies, waits for them, and re-layouts  47.8 us
    all_gather x4, waiting for transfers between devices, gather_ctx(): lax.all_gather(values.reshape(-1, values.shape[-1]), 'ctx', axis=0, tiled...  36.8 us
    pallas_call x1, Pallas kernels, attend(): pl.pallas_call(attend_kernel, grid_spec=pltpu.PrefetchScalarGridSpec(num_...  34.2 us
  transfers between devices with their start and end apart: 8, of which 1 were waited for; matrix products, arithmetic and copies ran while one was open for 25% of the time, Pallas kernels for 45%

profile of v3, /device:TPU:0, one launch (start us, length us, event | category | flops | bytes accessed | tf_op | source)
XLA Modules:
  0.0 1500.2 jit_solution(9234352399155443935)
XLA Ops:
  11.7 13.1 exchange_qkv.1
  37.8 42.1 %gather_normed.2 = (bf16[4,256,2048]{2,1,0:T(8,128)(2,1)}, bf16[256,2048]{1,0:T(8,128)(2,1)}, s32[4,32,128]{2,1,0:T(8,128)}) custom-call(bf16[256,2048]{1,0:T(8,128)(2,1)} %copy.209.refs_0_, bf16[256,2048]{1,0:T(8,128)(2,1)} %get-tuple-element.118.refs_1_, s32[32,128]{1,0:T(8,128)} %pad_bitcast_fusion.1.refs_2_, bf16[4,64,768]{2,1,0:T(8,128)(2,1)} %get-tuple-element.45.refs_3_), custom_call_target="tpu_custom_call" | custom-call | bytes 1048576 | tf_op jit(solution)/shard_map/gather_normed/pallas_call | solution.py:714
  100.3 60.6 %gather_normed.3 = (bf16[4,256,2048]{2,1,0:T(8,128)(2,1)}, bf16[256,2048]{1,0:T(8,128)(2,1)}, bf16[4,64,4096]{2,1,0:T(8,128)(2,1)}) custom-call(bf16[256,2048]{1,0:T(8,128)(2,1)} %copy.226.refs_0_, bf16[256,2048]{1,0:T(8,128)(2,1)} %get-tuple-element.121.refs_1_, bf16[4,64,4096]{2,1,0:T(8,128)(2,1)} %reshape.589.refs_2_), custom_call_target="tpu_custom_call" | custom-call | bytes 1048576 | tf_op jit(solution)/shard_map/gather_normed/pallas_call | solution.py:714
  165.1 6.5 fusion.29
  182.6 36.8 %all-gather.7.cloned.1.call-done.refs_2_ = bf16[2048,2048]{1,0:T(8,128)(2,1)} async-done(((bf16[256,2048]{1,0:T(8,128)(2,1)}), bf16[2048,2048]{1,0:T(8,128)(2,1)}) %all-gather.7.cloned.1.call-update) | async-done | bytes 8388624 | tf_op jit(solution)/shard_map/all_gather | solution.py:807
  219.3 123.9 %gather_keys.1 = (bf16[8,4096,128]{2,1,0:T(8,128)(2,1)}, bf16[4,512,2048]{2,1,0:T(8,128)(2,1)}) custom-call(bf16[4096,128]{1,0:T(8,128)(2,1)} %bitcast.289, bf16[512,2048]{1,0:T(8,128)(2,1)} %pad_maximum_fusion.8.refs_1_, bf16[2048,2048]{1,0:T(8,128)(2,1)} %all-gather.7.cloned.1.call-done.refs_2_), custom_call_target="tpu_custom_call" | custom-call | bytes 1048576 | tf_op jit(solution)/shard_map/gather_keys/pallas_call | solution.py:714
  377.0 34.2 %attend.1 = (bf16[8,256,512]{2,1,0:T(8,128)(2,1)S(1)}, f32[8,2,1,1024]{3,2,1,0:T(1,128)S(1)}) custom-call(s32[8,4]{1,0:T(8,128)S(1)} %pad_add_fusion.1.meta_ref, s32[8,1,1024]{2,1,0:T(1,128)S(1)} %tile.35.start_ref, s32[8,1,1024]{2,1,0:T(1,128)S(1)} %tile.37.index_ref, bf16[8,256,512]{2,1,0:T(8,128)(2,1)S(1)} %copy.232.query_ref, ...), custom_call_target="tpu_custom_call" | custom-call | flops 1073741824 | bytes 1048576 | tf_op jit(solution)/shard_map/attend/pallas_call | solution.py:190
  412.5 24.4 %fusion.74 = f32[2048,2048]{0,1:T(8,128)} fusion(bf16[2048,2048]{1,0:T(8,128)(2,1)} %bitcast.322, bf16[2048,2048]{1,0:T(8,128)(2,1)} %all-gather.7.cloned.1.call-done.refs_2_), kind=kOutput, calls=%fused_computation.211 | convolution fusion | flops 17179869184 | bytes 33554432 | tf_op jit(solution)/shard_map/dot_general | solution.py:59
  436.9 8.4 convolution_convert_fusion.2
  445.4 77.1 %sum_mixed.1 = f32[512,2048]{1,0:T(8,128)} custom-call(bf16[4,512,2048]{2,1,0:T(8,128)(2,1)} %bitcast.267), custom_call_target="tpu_custom_call" | custom-call | bytes 1048576 | tf_op jit(solution)/shard_map/sum_mixed/pallas_call | solution.py:714
  537.0 71.4 %gather_feed.1 = bf16[4,512,2048]{2,1,0:T(8,128)(2,1)} custom-call(bf16[512,2048]{1,0:T(8,128)(2,1)} %copy.235.refs_0_), custom_call_target="tpu_custom_call" | custom-call | bytes 1048576 | tf_op jit(solution)/shard_map/gather_feed/pallas_call | solution.py:714
  608.5 24.4 %fusion.2 = f32[2048,2048]{0,1:T(8,128)} fusion(bf16[2048,2048]{1,0:T(8,128)(2,1)} %bitcast.264, bf16[2048,4096]{1,0:T(8,128)(2,1)} %all-gather.11.cloned.1.call-done), kind=kOutput, calls=%fused_computation.8 | convolution fusion | flops 17179869184 | bytes 33554432 | tf_op jit(solution)/shard_map/dot_general | solution.py:59
  632.9 36.6 %multiply_convert_fusion.1 = (bf16[2048,2048]{0,1:T(8,128)(2,1)}, bf16[2048,2048]{0,1:T(8,128)(2,1)}, bf16[2048,2048]{0,1:T(8,128)(2,1)}) fusion(f32[2048,2048]{0,1:T(8,128)} %fusion.74, f32[2048,2048]{0,1:T(8,128)} %fusion.2, bf16[2048,2048]{1,0:T(8,128)(2,1)} %bitcast.265, bf16[2048,4096]{1,0:T(8,128)(2,1)} %all-gather.11.cloned.1.call-done), kind=kOutput, calls=%fused_computation.2 | convolution fusion | flops 17242783744 | bytes 75497472 | tf_op jit(solution)/shard_map/dot_general | solution.py:59
  669.5 43.4 %convolution_convert_fusion.refs_1_ = bf16[2048,4096]{1,0:T(8,128)(2,1)} fusion(bf16[2048,2048]{1,0:T(8,128)(2,1)} %bitcast.266, bf16[2048,2048]{0,1:T(8,128)(2,1)} %get-tuple-element.98, bf16[2048,2048]{0,1:T(8,128)(2,1)} %get-tuple-element.97), kind=kOutput, calls=%fused_computation.6 | convolution fusion | flops 34401681408 | bytes 41943040 | tf_op jit(solution)/shard_map/dot_general | solution.py:59
  713.0 45.3 %fusion.6 = bf16[2048,2048]{1,0:T(8,128)(2,1)} fusion(bf16[2048,4096]{1,0:T(8,128)(2,1)} %all-gather.11.cloned.1.call-done, bf16[2048,2048]{0,1:T(8,128)(2,1)} %get-tuple-element.98, bf16[2048,2048]{0,1:T(8,128)(2,1)} %get-tuple-element.97), kind=kOutput, calls=%fused_computation.15 | convolution fusion | flops 34397487104 | bytes 41943040 | tf_op jit(solution)/shard_map/dot_general | solution.py:59
  758.2 75.3 %sum_feed.1 = f32[512,2048]{1,0:T(8,128)} custom-call(bf16[4,512,2048]{2,1,0:T(8,128)(2,1)} %bitcast.262, bf16[2048,4096]{1,0:T(8,128)(2,1)} %convolution_convert_fusion.refs_1_), custom_call_target="tpu_custom_call" | custom-call | bytes 1048576 | tf_op jit(solution)/shard_map/sum_feed/pallas_call | solution.py:714
  860.4 69.8 %gather_middle.1 = bf16[4,512,2048]{2,1,0:T(8,128)(2,1)} custom-call(bf16[512,2048]{1,0:T(8,128)(2,1)} %get-tuple-element.88.refs_0_), custom_call_target="tpu_custom_call" | custom-call | bytes 1048576 | tf_op jit(solution)/shard_map/gather_middle/pallas_call | solution.py:714
  930.1 9.9 copy.283
  946.5 23.6 %select_select_fusion = bf16[2048,2048]{1,0:T(8,128)(2,1)} fusion(pred[]{:T(512)} %bitcast.61, pred[]{:T(512)} %bitcast.56, bf16[2048,2048]{0,1:T(8,128)(2,1)} %get-tuple-element.99, bf16[2048,2048]{1,0:T(8,128)(2,1)} %bitcast.323), kind=kOutput, calls=%fused_computation.12 | convolution fusion | flops 17192452096 | bytes 25165826 | tf_op jit(solution)/shard_map/dot_general | solution.py:59
  980.5 24.0 %convolution_convert_fusion.1 = bf16[2048,2048]{1,0:T(8,128)(2,1)} fusion(bf16[2048,2048]{0,1:T(8,128)(2,1)} %get-tuple-element.99, bf16[2048,2048]{1,0:T(8,128)(2,1)} %all-gather.7.cloned.1.call-done.refs_2_), kind=kOutput, calls=%fused_computation.13 | convolution fusion | flops 17184063488 | bytes 25165824 | tf_op jit(solution)/shard_map/dot_general | solution.py:59
  1004.5 10.1 convert_multiply_fusion.2
  1019.9 6.2 copy.282
  1032.2 72.8 %attend_back.1 = (f32[8,256,512]{2,1,0:T(8,128)S(1)}, bf16[8,8,2,256,128]{4,3,2,1,0:T(8,128)(2,1)}) custom-call(s32[8,4]{1,0:T(8,128)S(1)} %copy-done.7, s32[8,1,1024]{2,1,0:T(1,128)S(1)} %tile.35.start_ref, s32[8,1,1024]{2,1,0:T(1,128)S(1)} %tile.37.index_ref, bf16[8,256,512]{2,1,0:T(8,128)(2,1)S(1)} %copy-done.3, bf16[8,8,2,256,128]{4,3,2,1,0:T(8,128)(2,1)} %bitcast.233, ...), custom_call_target="tpu_custom_call" | custom-call | flops 2147483648 | bytes 1048576 | tf_op jit(solution)/shard_map/attend_back/pallas_call | solution.py:218
  1132.1 8.1 multiply_reduce_fusion
  1143.7 9.1 fusion.18
  1152.9 119.9 %sum_keys.1 = (f32[512,2048]{1,0:T(8,128)}, f32[4096,128]{1,0:T(8,128)}, bf16[4,64,4096]{2,1,0:T(8,128)(2,1)}) custom-call(bf16[4,512,2048]{2,1,0:T(8,128)(2,1)} %bitcast.268, bf16[8,4096,128]{2,1,0:T(8,128)(2,1)} %bitcast.269, bf16[4,64,4096]{2,1,0:T(8,128)(2,1)} %bitcast.236, bf16[256,2048]{1,0:T(8,128)(2,1)} %reduce-scatter.7.cloned.1.call-done.refs_3_), custom_call_target="tpu_custom_call" | custom-call | bytes 1048576 | tf_op jit(solution)/shard_map/sum_keys/pallas_call | solution.py:714
  1306.1 6.8 reshape.639
  1312.8 8.1 copy.270
  1321.0 6.1 reshape.638
  1329.1 7.2 convolution_convert_fusion.4
  1354.6 59.1 %sum_normed.2 = (f32[256,2048]{1,0:T(8,128)}, f32[8,8,128]{2,1,0:T(8,128)}, bf16[256,2048]{1,0:T(8,128)(2,1)}) custom-call(bf16[4,256,2048]{2,1,0:T(8,128)(2,1)} %bitcast.288, f32[8,128]{1,0:T(8,128)} %pad_bitcast_fusion.2.refs_1_, bf16[256,2048]{1,0:T(8,128)(2,1)} %get-tuple-element.116.refs_2_, bf16[2048,768]{1,0:T(8,128)(2,1)} %add_convert_fusion.refs_3_, ...), custom_call_target="tpu_custom_call" | custom-call | bytes 1048576 | tf_op jit(solution)/shard_map/sum_normed/pallas_call | solution.py:714
  1426.4 47.4 %sum_normed.3 = (f32[256,2048]{1,0:T(8,128)}, f32[4,32,128]{2,1,0:T(8,128)}, bf16[256,2048]{1,0:T(8,128)(2,1)}, bf16[4,64,768]{2,1,0:T(8,128)(2,1)}) custom-call(bf16[4,256,2048]{2,1,0:T(8,128)(2,1)} %bitcast.281, f32[32,128]{1,0:T(8,128)} %pad_bitcast_fusion.refs_1_, bf16[256,2048]{1,0:T(8,128)(2,1)} %fusion.21.refs_2_, bf16[4,64,768]{2,1,0:T(8,128)(2,1)} %bitcast.306), custom_call_target="tpu_custom_call" | custom-call | bytes 1048576 | tf_op jit(solution)/shard_map/sum_normed/pallas_call | solution.py:714
  (397 shorter events, 267.1 us)
Async XLA Ops:
  7.2 157.9 %all-gather.5.cloned.1.call-start = ((), (), s32[]{:S(2)}) async-start(), calls=%async_computation.4 | async-start | bytes 3538944 | tf_op jit(solution)/shard_map/all_gather | solution.py:807
  8.0 77.5 %copy-start.80 = (f32[64]{0:T(128)}, f32[64]{0:T(128)S(1)}, u32[]{:S(2)}) copy-start(f32[64]{0:T(128)S(1)} %get-tuple-element.141) | copy-start | bytes 772
  8.0 19.7 %copy-start.33 = (bf16[2,256,2048]{2,1,0:T(8,128)(2,1)S(1)}, bf16[2,256,2048]{2,1,0:T(8,128)(2,1)}, u32[]{:S(2)}) copy-start(bf16[2,256,2048]{2,1,0:T(8,128)(2,1)} %param.22) | copy-start | bytes 6291460
  24.8 194.5 %all-gather.7.cloned.1.call-start = ((), (), s32[]{:S(2)}) async-start(), calls=%async_computation.5 | async-start | bytes 9437184 | tf_op jit(solution)/shard_map/all_gather | solution.py:807
  27.6 409.3 %all-gather.9.cloned.1.call-start = ((), (), s32[]{:S(2)}) async-start(), calls=%async_computation.6 | async-start | bytes 2359296 | tf_op jit(solution)/shard_map/all_gather | solution.py:807
  97.5 63.4 %copy-start.84 = (f32[2,64]{1,0:T(2,128)S(1)}, f32[2,64]{1,0:T(2,128)}, u32[]{:S(2)}) copy-start(f32[2,64]{1,0:T(2,128)} %param.41) | copy-start | bytes 1540
  100.3 61.8 %copy-start.29 = (bf16[256,2048]{1,0:T(8,128)(2,1)}, bf16[256,2048]{1,0:T(8,128)(2,1)S(1)}, u32[]{:S(2)}) copy-start(bf16[256,2048]{1,0:T(8,128)(2,1)S(1)} %get-tuple-element.120) | copy-start | bytes 3145732
  160.9 19.3 %copy-start.82 = (f32[64]{0:T(128)}, f32[64]{0:T(128)S(1)}, u32[]{:S(2)}) copy-start(f32[64]{0:T(128)S(1)} %get-tuple-element.139) | copy-start | bytes 772
  161.0 204.9 %copy-start.76 = (f32[64]{0:T(128)}, f32[64]{0:T(128)S(1)}, u32[]{:S(2)}) copy-start(f32[64]{0:T(128)S(1)} %get-tuple-element.140) | copy-start | bytes 772
  162.0 205.3 %copy-start.38 = (f32[8,256,32]{1,2,0:T(8,128)}, f32[8,256,32]{1,2,0:T(8,128)S(1)}, u32[]{:S(2)}) copy-start(f32[8,256,32]{1,2,0:T(8,128)S(1)} %get-tuple-element.135) | copy-start | bytes 786436
  162.0 205.3 %copy-start.40 = (f32[8,256,32]{1,2,0:T(8,128)}, f32[8,256,32]{1,2,0:T(8,128)S(1)}, u32[]{:S(2)}) copy-start(f32[8,256,32]{1,2,0:T(8,128)S(1)} %get-tuple-element.136) | copy-start | bytes 786436
  219.3 126.5 %copy-start.48 = (f32[64,2048]{1,0:T(8,128)S(1)}, f32[64,2048]{1,0:T(8,128)}, u32[]{:S(2)}) copy-start(f32[64,2048]{1,0:T(8,128)} %param.29) | copy-start | bytes 1572868
  346.6 261.9 %all-gather.11.cloned.1.call-start = ((), (), s32[]{:S(2)}) async-start(), calls=%async_computation.7 | async-start | bytes 18874368 | tf_op jit(solution)/shard_map/all_gather | solution.py:807
  349.8 592.8 %reduce-scatter.5.cloned.1.call-start = ((), (), s32[]{:S(2)}) async-start(), calls=%async_computation.8 | async-start | bytes 18874368 | tf_op jit(solution)/shard_map/reduce_scatter | solution.py:810
  352.2 20.6 %copy-start.6 = (s32[8,4]{1,0:T(8,128)}, s32[8,4]{1,0:T(8,128)S(1)}, u32[]{:S(2)}) copy-start(s32[8,4]{1,0:T(8,128)S(1)} %pad_add_fusion.1.meta_ref) | copy-start | bytes 388
  372.8 38.3 %copy-start.2 = (bf16[8,256,512]{2,1,0:T(8,128)(2,1)}, bf16[8,256,512]{2,1,0:T(8,128)(2,1)S(1)}, u32[]{:S(2)}) copy-start(bf16[8,256,512]{2,1,0:T(8,128)(2,1)S(1)} %copy.232.query_ref) | copy-start | bytes 6291460
  412.5 24.4 %copy-start.9 = (bf16[8,256,512]{2,1,0:T(8,128)(2,1)S(1)}, bf16[8,256,512]{2,1,0:T(8,128)(2,1)}, u32[]{:S(2)}) copy-start(bf16[8,256,512]{2,1,0:T(8,128)(2,1)} %copy-done.8) | copy-start | bytes 6291460
  445.3 77.1 %copy-start.35 = (f32[256,2048]{1,0:T(8,128)S(1)}, f32[256,2048]{1,0:T(8,128)}, u32[]{:S(2)}) copy-start(f32[256,2048]{1,0:T(8,128)} %get-tuple-element.117) | copy-start | bytes 6291460
  445.4 77.1 %copy-start.37 = (f32[256,2048]{1,0:T(8,128)S(1)}, f32[256,2048]{1,0:T(8,128)}, u32[]{:S(2)}) copy-start(f32[256,2048]{1,0:T(8,128)} %convert_element_type.171) | copy-start | bytes 6291460
  712.9 427.4 %reduce-scatter.7.cloned.1.call-start = ((), (), s32[]{:S(2)}) async-start(), calls=%async_computation.9 | async-start | bytes 9437184 | tf_op jit(solution)/shard_map/reduce_scatter | solution.py:810
  843.9 9.7 copy-start.30
  843.9 9.7 copy-start.44
  970.1 384.5 %reduce-scatter.9.cloned.1.call-start = ((), (), s32[]{:S(2)}) async-start(), calls=%async_computation.10 | async-start | bytes 2359296 | tf_op jit(solution)/shard_map/reduce_scatter | solution.py:810
  980.5 24.0 %copy-start.10 = (bf16[8,256,512]{2,1,0:T(8,128)(2,1)S(1)}, bf16[8,256,512]{2,1,0:T(8,128)(2,1)}, u32[]{:S(2)}) copy-start(bf16[8,256,512]{2,1,0:T(8,128)(2,1)} %copy-done.8) | copy-start | bytes 6291460
  980.5 24.0 %copy-start.97 = (bf16[512,2048]{1,0:T(8,128)(2,1)S(1)}, bf16[512,2048]{1,0:T(8,128)(2,1)}, u32[]{:S(2)}) copy-start(bf16[512,2048]{1,0:T(8,128)(2,1)} %all-gather.9.cloned.1.call-done) | copy-start | bytes 6291460
  1132.1 11.5 copy-start.11
  1152.8 273.5 %reduce-scatter.11.cloned.1.call-start = ((), (), s32[]{:S(2)}) async-start(), calls=%async_computation.11 | async-start | bytes 3538944 | tf_op jit(solution)/shard_map/reduce_scatter | solution.py:810
  1279.3 7.3 copy-start.42
  1281.8 7.8 copy-start.32
  1291.5 9.2 copy-start.55
  1329.1 7.2 copy-start.96
  1336.3 9.2 copy-start.46
  (74 other events, 285.8 us)
Sparse Core Ops, SparseCore 0:
  24.9 67.9 all-gather.4
  95.1 124.2 all-gather.6
  346.8 27.2 all-gather.8
  376.1 150.5 all-gather.10
  713.0 165.4 reduce-scatter.4
  970.2 86.7 reduce-scatter.6
  1152.9 35.5 reduce-scatter.8
  1306.1 43.9 reduce-scatter.10
